TPU v7x, 32 devices: a whole 2x2x4 slice. The times are simulated.
32 devices in a mesh: dp: 2 (over x), seq: 4 (over y, core), mp: 4 (over z).
Axes of the slice: x: 2, y: 2, z: 4, core: 2. Of those that a mesh axis runs over, the one named last changes fastest.
Arguments:
- spectrogram: bfloat16 [2, 4096, 80], P('dp', 'seq'), may hold values from -6 to 6
- first_kernel: bfloat16 [3, 80, 768], P(None, None, 'mp'), may hold values from -0.375 to 0.375
- first_bias: float32 [768], P('mp'), may hold values from -3 to 3
- second_kernel: bfloat16 [3, 768, 768], P(None, 'mp'), may hold values from -0.125 to 0.125
- second_bias: float32 [768], replicated, may hold values from -3 to 3
- attend_gain: float32 [768], replicated, may hold values from 0.25 to 1.75
- attend_shift: float32 [768], replicated, may hold values from -2 to 2
- project_weight: bfloat16 [768, 3, 768], P(None, None, 'mp'), may hold values from -0.21875 to 0.21875
- project_bias: float32 [2, 768], P(None, 'mp'), may hold values from -2 to 2
- output_weight: bfloat16 [768, 768], P('mp'), may hold values from -1.75 to 1.75
- output_bias: float32 [768], replicated, may hold values from -2 to 2
- mixer_gain: float32 [768], replicated, may hold values from 0.25 to 1.75
- mixer_shift: float32 [768], replicated, may hold values from -2 to 2
- expand_weight: bfloat16 [768, 3072], P(None, 'mp'), may hold values from -0.21875 to 0.21875
- expand_bias: float32 [3072], P('mp'), may hold values from -2 to 2
- reduce_weight: bfloat16 [3072, 768], P('mp'), may hold values from -0.109375 to 0.109375
- reduce_bias: float32 [768], replicated, may hold values from -2 to 2
- cotangent: float32 [2, 2048, 768], P('dp', 'seq'), may hold values from -6 to 6
Outputs:
- encoded: float32 [2, 2048, 768], P('dp', 'seq')
- spectrogram_gradient: float32 [2, 4096, 80], P('dp', 'seq')
- first_kernel_gradient: float32 [3, 80, 768], P(None, None, 'mp')
- first_bias_gradient: float32 [768], P('mp')
- second_kernel_gradient: float32 [3, 768, 768], P(None, 'mp')
- second_bias_gradient: float32 [768], replicated
- attend_gain_gradient: float32 [768], replicated
- attend_shift_gradient: float32 [768], replicated
- project_weight_gradient: float32 [768, 3, 768], P(None, None, 'mp')
- project_bias_gradient: float32 [2, 768], P(None, 'mp')
- output_weight_gradient: float32 [768, 768], P('mp')
- output_bias_gradient: float32 [768], replicated
- mixer_gain_gradient: float32 [768], replicated
- mixer_shift_gradient: float32 [768], replicated
- expand_weight_gradient: float32 [768, 3072], P(None, 'mp')
- expand_bias_gradient: float32 [3072], P('mp')
- reduce_weight_gradient: float32 [3072, 768], P('mp')
- reduce_bias_gradient: float32 [768], replicated
All inputs are finite; a program needn't handle non-finite values.
Results may differ from a plain program's by a relative error of at most 0.015.
Values may be sent and summed in bfloat16 or wider, within the bound.
No kernel may reach another device: no remote copies, remote signals or barrier semaphores. Data moves between devices by JAX's collectives and lax.ppermute only.
A program may use at most 128 MiB of HBM per device.

v0:
```python
import math

import jax
import jax.numpy as jnp
from jax import lax
from jax.sharding import PartitionSpec as P

HEAD_DIM = 64


def with_halo(shard, sides, width):
    for axis, dim in sides:
        size, length = (lax.axis_size(axis), shard.shape[dim])
        up = [(i, (i + 1) % size) for i in range(size - 1)]
        down = [(j, i) for i, j in up]
        last = lax.slice_in_dim(shard, length - width, length, axis=dim)
        initial = lax.slice_in_dim(shard, 0, width, axis=dim)
        before = lax.ppermute(last, axis, up)
        after = lax.ppermute(initial, axis, down)
        shard = jnp.concatenate([before, shard, after], axis=dim)
    return shard


def passed_along(shard, axis, by):
    size = lax.axis_size(axis)
    pairs = [(i, i + by) for i in range(size) if 0 <= i + by < size]
    return lax.ppermute(shard, axis, pairs)


def exact_gelu(value):
    return jax.nn.gelu(value, approximate=False)


def gelu_back(value, grad):
    return jax.vjp(exact_gelu, value)[1](grad)[0]


def layer_norm(value, gain, shift):
    centre = value - jnp.mean(value, axis=-1, keepdims=True)
    spread = jnp.mean(centre * centre, axis=-1, keepdims=True)
    return centre * lax.rsqrt(spread + 1e-05) * gain + shift


def norm_back(value, gain, shift, grad):
    return jax.vjp(layer_norm, value, gain, shift)[1](grad)


def product(left, right):
    return jnp.dot(left, right, preferred_element_type=jnp.float32)


def column_total(value):
    return jnp.sum(value.astype(jnp.float32), axis=0)


def sinusoid(start, count, width):
    half = width // 2
    rates = jnp.exp(jnp.arange(half, dtype=jnp.float32) * (-math.log(10000.0) / (half - 1)))
    times = (start + jnp.arange(count)).astype(jnp.float32)
    angles = times[:, None] * rates[None, :]
    return jnp.concatenate([jnp.sin(angles), jnp.cos(angles)], axis=1)


def on_device(
    spectrogram,
    first_kernel,
    first_bias,
    second_kernel,
    second_bias,
    attend_gain,
    attend_shift,
    project_weight,
    project_bias,
    output_weight,
    output_bias,
    mixer_gain,
    mixer_shift,
    expand_weight,
    expand_bias,
    reduce_weight,
    reduce_bias,
    cotangent,
):
    clips, steps, bands = spectrogram.shape
    frames = steps // 2
    local_width = first_kernel.shape[2]
    model_width = second_kernel.shape[2]
    heads_here = local_width // HEAD_DIM
    whole_frames = frames * lax.axis_size("seq")
    rows = clips * frames
    scale = HEAD_DIM ** (-0.5)
    bf = jnp.bfloat16
    padded = with_halo(spectrogram, (("seq", 1),), 2)
    taps = jnp.concatenate([padded[:, index : index + steps + 1] for index in range(3)], axis=2)
    first_matrix = first_kernel.reshape(3 * bands, local_width)
    pre_one = (
        product(taps.reshape(-1, 3 * bands), first_matrix).reshape(clips, steps + 1, local_width)
        + first_bias
    )
    hidden_pad = exact_gelu(pre_one).astype(bf)
    position = jnp.arange(steps + 1)
    live = jnp.logical_or(position > 0, lax.axis_index("seq") > 0)
    hidden_pad = jnp.where(live[None, :, None], hidden_pad, jnp.zeros_like(hidden_pad))
    pre_local = pre_one[:, 1:]
    taps_two = jnp.concatenate(
        [hidden_pad[:, index : index + steps : 2] for index in range(3)], axis=2
    )
    taps_flat = taps_two.reshape(rows, 3 * local_width)
    second_matrix = second_kernel.reshape(3 * local_width, model_width)
    stem_pre = lax.psum(product(taps_flat, second_matrix), "mp") + second_bias
    table = jnp.tile(sinusoid(lax.axis_index("seq") * frames, frames, model_width), (clips, 1))
    resid_zero = exact_gelu(stem_pre) + table
    normed_one = layer_norm(resid_zero, attend_gain, attend_shift).astype(bf)
    project_matrix = project_weight.reshape(model_width, 3 * local_width)
    packed = product(normed_one, project_matrix).reshape(rows, 3, local_width)
    offsets = jnp.stack([project_bias[0], jnp.zeros_like(project_bias[0]), project_bias[1]])
    packed = (packed + offsets[None]).astype(bf)
    query = packed[:, 0].reshape(clips, frames, heads_here, HEAD_DIM)
    local_keys = packed[:, 1].reshape(clips, frames, local_width)
    local_values = packed[:, 2].reshape(clips, frames, local_width)
    all_keys, all_values = (
        lax.all_gather(local_keys, "seq", axis=1, tiled=True),
        lax.all_gather(local_values, "seq", axis=1, tiled=True),
    )
    all_keys = all_keys.reshape(clips, whole_frames, heads_here, HEAD_DIM)
    all_values = all_values.reshape(clips, whole_frames, heads_here, HEAD_DIM)
    scores = (
        jnp.einsum("cqhd,ckhd->chqk", query, all_keys, preferred_element_type=jnp.float32) * scale
    )
    soft = jax.nn.softmax(scores, axis=-1)
    soft_low = soft.astype(bf)
    attended = jnp.einsum(
        "chqk,ckhd->cqhd", soft_low, all_values, preferred_element_type=jnp.float32
    )
    attended = attended.astype(bf).reshape(rows, local_width)
    resid_one = resid_zero + lax.psum(product(attended, output_weight), "mp") + output_bias
    normed_two = layer_norm(resid_one, mixer_gain, mixer_shift).astype(bf)
    expanded = product(normed_two, expand_weight) + expand_bias
    active = exact_gelu(expanded).astype(bf)
    encoded = (
        resid_one
        + lax.psum(product(active, reduce_weight).astype(jnp.bfloat16), "mp").astype(jnp.float32)
        + reduce_bias
    )
    grad_out = cotangent.reshape(rows, model_width)
    grad_mlp = grad_out.astype(bf)
    reduce_bias_gradient = column_total(grad_mlp)
    reduce_weight_gradient = product(active.T, grad_mlp)
    grad_expanded = gelu_back(expanded, product(grad_mlp, reduce_weight.T)).astype(bf)
    expand_bias_gradient = column_total(grad_expanded)
    expand_weight_gradient = product(normed_two.T, grad_expanded)
    grad_normed_two = lax.psum(product(grad_expanded, expand_weight.T), "mp")
    back_two, mixer_gain_gradient, mixer_shift_gradient = norm_back(
        resid_one, mixer_gain, mixer_shift, grad_normed_two
    )
    grad_resid_one = grad_out + back_two
    grad_attn = grad_resid_one.astype(bf)
    output_bias_gradient = column_total(grad_attn)
    output_weight_gradient = product(attended.T, grad_attn)
    grad_attended = (
        product(grad_attn, output_weight.T).astype(bf).reshape(clips, frames, heads_here, HEAD_DIM)
    )
    grad_soft = jnp.einsum(
        "cqhd,ckhd->chqk", grad_attended, all_values, preferred_element_type=jnp.float32
    )
    values_full = jnp.einsum(
        "chqk,cqhd->ckhd", soft_low, grad_attended, preferred_element_type=jnp.float32
    )
    grad_scores = soft * (grad_soft - jnp.sum(soft * grad_soft, axis=-1, keepdims=True))
    grad_scores = grad_scores.astype(bf)
    query_grad = (
        jnp.einsum("chqk,ckhd->cqhd", grad_scores, all_keys, preferred_element_type=jnp.float32)
        * scale
    )
    keys_full = (
        jnp.einsum("chqk,cqhd->ckhd", grad_scores, query, preferred_element_type=jnp.float32)
        * scale
    )
    keys_grad, values_grad = (
        lax.psum_scatter(
            keys_full.reshape(clips, whole_frames, local_width),
            "seq",
            scatter_dimension=1,
            tiled=True,
        ),
        lax.psum_scatter(
            values_full.reshape(clips, whole_frames, local_width),
            "seq",
            scatter_dimension=1,
            tiled=True,
        ),
    )
    grad_packed = jnp.stack(
        [
            query_grad.reshape(rows, local_width),
            keys_grad.reshape(rows, local_width),
            values_grad.reshape(rows, local_width),
        ],
        axis=1,
    ).astype(bf)
    project_bias_gradient = jnp.stack(
        [column_total(grad_packed[:, 0]), column_total(grad_packed[:, 2])]
    )
    grad_packed_flat = grad_packed.reshape(rows, 3 * local_width)
    project_weight_gradient = product(normed_one.T, grad_packed_flat).reshape(
        model_width, 3, local_width
    )
    grad_normed_one = lax.psum(product(grad_packed_flat, project_matrix.T), "mp")
    back_one, attend_gain_gradient, attend_shift_gradient = norm_back(
        resid_zero, attend_gain, attend_shift, grad_normed_one
    )
    grad_resid_zero = grad_resid_one + back_one
    grad_stem = gelu_back(stem_pre, grad_resid_zero).astype(bf)
    second_bias_gradient = column_total(grad_stem)
    second_kernel_gradient = product(taps_flat.T, grad_stem).reshape(3, local_width, model_width)
    grad_taps = product(grad_stem, second_matrix.T).reshape(clips, frames, 3, local_width)
    following = passed_along(grad_stem.reshape(clips, frames, model_width)[:, 0:1], "seq", -1)
    edge = product(following.reshape(clips, model_width), second_kernel[0].T).reshape(
        clips, 1, local_width
    )
    shifted_zero = jnp.concatenate([grad_taps[:, 1:, 0], edge], axis=1)
    grad_odd = grad_taps[:, :, 2] + shifted_zero
    grad_hidden = jnp.stack([grad_taps[:, :, 1], grad_odd], axis=2).reshape(
        clips, steps, local_width
    )
    grad_pre = gelu_back(pre_local, grad_hidden).astype(bf)
    first_bias_gradient = column_total(grad_pre.reshape(-1, local_width))
    own_taps = taps[:, 1:].reshape(-1, 3 * bands)
    first_kernel_gradient = product(own_taps.T, grad_pre.reshape(-1, local_width)).reshape(
        3, bands, local_width
    )
    grad_rim = with_halo(grad_pre, (("seq", 1),), 1)
    back_taps = jnp.concatenate(
        [grad_rim[:, 2 : steps + 2], grad_rim[:, 1 : steps + 1], grad_rim[:, 0:steps]], axis=2
    )
    back_matrix = jnp.transpose(first_kernel, (0, 2, 1)).reshape(3 * local_width, bands)
    spectrogram_gradient = lax.psum(
        product(back_taps.reshape(-1, 3 * local_width), back_matrix), "mp"
    ).reshape(clips, steps, bands)
    totals = lax.psum(
        (
            first_kernel_gradient,
            first_bias_gradient,
            second_kernel_gradient,
            second_bias_gradient,
            attend_gain_gradient,
            attend_shift_gradient,
            project_weight_gradient,
            project_bias_gradient,
            output_weight_gradient,
            output_bias_gradient,
            mixer_gain_gradient,
            mixer_shift_gradient,
            expand_weight_gradient,
            expand_bias_gradient,
            reduce_weight_gradient,
            reduce_bias_gradient,
        ),
        ("dp", "seq"),
    )
    return (
        encoded.reshape(clips, frames, model_width),
        spectrogram_gradient,
        totals[0],
        totals[1],
        totals[2],
        totals[3],
        totals[4],
        totals[5],
        totals[6],
        totals[7],
        totals[8],
        totals[9],
        totals[10],
        totals[11],
        totals[12],
        totals[13],
        totals[14],
        totals[15],
    )


def solution(mesh):
    return jax.shard_map(
        on_device,
        mesh=mesh,
        in_specs=(
            P("dp", "seq", None),
            P(None, None, "mp"),
            P("mp"),
            P(None, "mp", None),
            P(),
            P(),
            P(),
            P(None, None, "mp"),
            P(None, "mp"),
            P("mp", None),
            P(),
            P(),
            P(),
            P(None, "mp"),
            P("mp"),
            P("mp", None),
            P(),
            P("dp", "seq", None),
        ),
        out_specs=(
            P("dp", "seq", None),
            P("dp", "seq", None),
            P(None, None, "mp"),
            P("mp"),
            P(None, "mp", None),
            P(),
            P(),
            P(),
            P(None, None, "mp"),
            P(None, "mp"),
            P("mp", None),
            P(),
            P(),
            P(),
            P(None, "mp"),
            P("mp"),
            P("mp", None),
            P(),
        ),
        check_vma=False,
    )
```

profile of v0, /device:TPU:0, one launch (start us, length us, event | category | flops | bytes accessed | tf_op | source)
XLA Modules:
  0.0 749.1 jit_solution(9440668534995953624)
XLA Ops:
  8.2 2.3 collective-permute-start
  10.5 1.3 collective-permute-start.1
  12.9 2.8 collective-permute-done.1
  16.3 1.5 convolution_add_fusion
  17.8 1.9 select_bitcast_fusion
  19.8 8.1 %slice.88 = bf16[1,512,192]{1,2,0:T(8,128)(2,1)S(1)} slice(bf16[1,1025,192]{1,2,0:T(8,128)(2,1)S(1)} %select_bitcast_fusion), slice={[0:1:1], [0:1024:2], [0:192:1]} | slice | bytes 393216 | tf_op jit(solution)/shard_map/slice | solution.py:106
  27.9 8.1 %slice.89 = bf16[1,512,192]{1,2,0:T(8,128)(2,1)S(1)} slice(bf16[1,1025,192]{1,2,0:T(8,128)(2,1)S(1)} %select_bitcast_fusion), slice={[0:1:1], [1:1025:2], [0:192:1]} | slice | bytes 393216 | tf_op jit(solution)/shard_map/slice | solution.py:106
  36.0 8.2 %slice.90 = bf16[1,512,192]{1,2,0:T(8,128)(2,1)S(1)} slice(bf16[1,1025,192]{1,2,0:T(8,128)(2,1)S(1)} %select_bitcast_fusion), slice={[0:1:1], [2:1025:2], [0:192:1]} | slice | bytes 393216 | tf_op jit(solution)/shard_map/slice | solution.py:106
  44.2 3.2 fusion.64
  48.7 3.8 multiply_sine_fusion
  52.5 66.7 %all-reduce.10.cloned.1.call-done = f32[512,768]{1,0:T(8,128)} async-done(((f32[512,768]{1,0:T(8,128)}), f32[512,768]{1,0:T(8,128)}) %all-reduce.10.cloned.1.call-update) | async-done | bytes 1572880 | tf_op jit(solution)/shard_map/psum | solution.py:110
  119.1 5.0 fusion.95
  126.9 8.6 %all-gather.1 = bf16[2048,1,192]{0,2,1:T(8,128)(2,1)S(1)} all-gather(bf16[512,1,192]{0,2,1:T(8,128)(2,1)S(1)} %get-tuple-element.61), channel_id=3, replica_groups=mesh['dp'=2,'seq'=4,'mp'=4] {'seq'}, dimensions={0}, use_global_device_ids=true | all-gather | bytes 983040 | tf_op jit(solution)/shard_map/all_gather | solution.py:122
  135.5 9.2 %all-gather = bf16[2048,1,192]{0,2,1:T(8,128)(2,1)} all-gather(bf16[512,1,192]{0,2,1:T(8,128)(2,1)S(1)} %get-tuple-element.63), channel_id=2, replica_groups=mesh['dp'=2,'seq'=4,'mp'=4] {'seq'}, dimensions={0}, use_global_device_ids=true | all-gather | bytes 983040 | tf_op jit(solution)/shard_map/all_gather | solution.py:123
  144.7 9.7 %fusion.101 = (f32[3,512]{1,0:T(4,128)}, f32[3,512,2048]{2,1,0:T(8,128)}) fusion(bf16[512,3,64]{0,2,1:T(8,128)(2,1)} %bitcast.187, bf16[2048,3,64]{0,2,1:T(8,128)(2,1)S(1)} %bitcast.177), kind=kOutput, calls=%fused_computation.188 | convolution fusion | flops 412092416 | bytes 13572096 | tf_op jit(solution)/shard_map/sub | solution.py:130
  154.4 6.8 fusion.32
  161.9 1.6 fusion.107
  163.8 67.9 %all-reduce.12.cloned.1.call-done = f32[512,768]{1,0:T(8,128)} async-done(((f32[512,768]{1,0:T(8,128)}), f32[512,768]{1,0:T(8,128)}) %all-reduce.12.cloned.1.call-update) | async-done | bytes 1572880 | tf_op jit(solution)/shard_map/psum | solution.py:136
  231.6 1.7 fusion.94
  234.4 5.1 multiply_convert_fusion.1
  239.5 1.8 convert_reduce_fusion.1
  242.2 2.0 fusion.108
  244.3 1.1 copy-done.28
  245.3 3.0 convolution_convert_fusion
  248.4 64.1 %all-reduce.16.cloned.1.call-done = f32[512,768]{1,0:T(8,128)} async-done(((f32[512,768]{1,0:T(8,128)}), f32[512,768]{1,0:T(8,128)}) %all-reduce.16.cloned.1.call-update) | async-done | bytes 1572880 | tf_op jit(solution)/shard_map/psum | solution.py:152
  312.6 3.1 multiply_reduce_fusion.2
  315.7 42.4 %all-reduce.14.cloned.1.call-done = bf16[512,768]{1,0:T(8,128)(2,1)} async-done(((bf16[512,768]{1,0:T(8,128)(2,1)}), bf16[512,768]{1,0:T(8,128)(2,1)}) %all-reduce.14.cloned.1.call-update) | async-done | bytes 786448 | tf_op jit(solution)/shard_map/psum | solution.py:142
  358.1 4.0 fusion.92
  363.9 10.3 %multiply_reduce_fusion = (f32[3,512]{1,0:T(4,128)S(1)}, f32[3,512,2048]{2,1,0:T(8,128)}) fusion(f32[3,512,2048]{2,1,0:T(8,128)} %get-tuple-element.73, f32[3,512]{1,0:T(4,128)S(1)} %copy-done.68, bf16[512,3,64]{0,2,1:T(8,128)(2,1)S(1)} %bitcast.192, bf16[2048,3,64]{0,2,1:T(8,128)(2,1)S(1)} %bitcast.184), kind=kOutput, calls=%fused_computation.2 | convolution fusion | flops 412088832 | bytes 26161152 | tf_op jit(solution)/shard_map/cqhd,ckhd->chqk/dot_general | solution.py:163
  375.3 1.2 slice-done.2
  376.5 6.0 multiply_convert_fusion
  382.4 2.8 convolution_multiply_fusion
  386.5 7.3 fusion.7
  394.0 4.8 convolution_multiply_fusion.1
  398.9 14.3 %reduce-scatter.3.cloned.1.call-done = f32[1,512,192]{1,2,0:T(8,128)} async-done(((f32[1,2048,192]{1,2,0:T(8,128)}), f32[1,512,192]{1,2,0:T(8,128)}) %reduce-scatter.3.cloned.1.call-update) | async-done | bytes 393232 | tf_op jit(solution)/shard_map/reduce_scatter | solution.py:180
  413.2 31.4 %reduce-scatter.5.cloned.1.call-done = f32[1,512,192]{1,2,0:T(8,128)} async-done(((f32[1,2048,192]{1,2,0:T(8,128)}), f32[1,512,192]{1,2,0:T(8,128)}) %reduce-scatter.5.cloned.1.call-update) | async-done | bytes 393232 | tf_op jit(solution)/shard_map/reduce_scatter | solution.py:186
  444.6 1.2 maximum_convert_fusion
  446.6 3.1 convolution_bitcast_fusion
  449.9 1.2 copy.41
  453.9 2.2 fusion.102
  456.1 2.4 fusion.86
  458.5 1.2 fusion.109
  459.7 59.4 %all-reduce.18.cloned.1.call-done = f32[512,768]{1,0:T(8,128)} async-done(((f32[512,768]{1,0:T(8,128)}), f32[512,768]{1,0:T(8,128)}) %all-reduce.18.cloned.1.call-update) | async-done | bytes 1572880 | tf_op jit(solution)/shard_map/psum | solution.py:208
  519.0 2.5 fusion.87
  523.5 5.4 convert_reduce_fusion.3
  528.9 1.3 collective-permute-start.2
  532.4 1.9 copy.38
  534.3 2.3 copy.39
  536.7 3.3 convert_reduce_fusion.4
  540.1 1.3 collective-permute-start.3
  541.4 4.7 collective-permute-start.4
  546.1 2.0 fusion.62
  548.2 1.2 convolution_bitcast_fusion.2
  549.5 1.8 fusion.52
  553.7 25.3 %all-reduce = (f32[192]{0:T(256)}, f32[768]{0:T(1024)}, f32[768]{0:T(1024)}, f32[768]{0:T(1024)}, f32[2,192]{1,0:T(2,128)}, /*index=5*/f32[768]{0:T(1024)}, f32[...) all-reduce(f32[192]{0:T(256)S(1)} %get-tuple-element.47, ...), channel_id=1, replica_groups=mesh['dp'=2,'seq'=4,'mp'=4] {'dp','seq'}, use_global_device_ids=true, to_apply=%region_21.22 | all-reduce | flops 6720 | bytes 53760 | tf_op jit(solution)/shard_map/psum | solution.py:240
  579.0 7.3 all-reduce.20.cloned.1.call-done
  586.3 142.9 %all-reduce.22.cloned.1.call-done = (f32[3,80,192]{2,1,0:T(8,128)}, f32[3,192,768]{2,1,0:T(8,128)}, f32[768,3,192]{0,2,1:T(8,128)}, f32[192,768]{1,0:T(8,128)}, f32[768,768]{1,0:T(8,128)}, /*index=5*/f32[768,768]{1,0:T(8,128)}) async-done(((f32[3,80,192]{2,1,0:T(8,128)}, f32[3,192,768]{2,1,0:T(8,128)}, f32[768,3,192]{0,2,1:T(8,128)}, f32[192,768]{1,0:T(8,128)}, f32[768,768]{1,0:T(8,128)}, ...) | async-done | bytes 9031696 | tf_op jit(solution)/shard_map/psum | solution.py:240
  729.2 1.7 copy.54
  730.9 1.7 copy.55
  732.5 2.9 copy.56
  735.5 1.2 copy.57
  738.1 1.4 copy.59
  739.6 1.1 copy-done.14
  740.7 1.4 copy.60
  (230 shorter events, 25.6 us)
Async XLA Ops:
  7.2 227.2 %copy-start = (bf16[768,768]{1,0:T(8,128)(2,1)S(1)}, bf16[768,768]{1,0:T(8,128)(2,1)}, u32[]{:S(2)}) copy-start(bf16[768,768]{1,0:T(8,128)(2,1)} %param.31) | copy-start | bytes 3538948
  7.2 111.9 %all-reduce.10.cloned.1.call-start = ((), (), s32[]{:S(2)}) async-start(), calls=%async_computation.2 | async-start | bytes 3145728 | tf_op jit(solution)/shard_map/psum | solution.py:110
  8.2 3.7 collective-permute-start
  10.5 5.2 collective-permute-start.1
  11.8 3.9 copy-start.46
  12.9 2.8 copy-start.40
  17.8 29.5 %copy-start.13 = (f32[1025,192]{0,1:T(8,128)}, f32[1025,192]{0,1:T(8,128)S(1)}, u32[]{:S(2)}) copy-start(f32[1025,192]{0,1:T(8,128)S(1)} %convolution_add_fusion) | copy-start | bytes 2361604
  27.9 19.5 %copy-start.30 = (bf16[1,512,192]{1,2,0:T(8,128)(2,1)}, bf16[1,512,192]{1,2,0:T(8,128)(2,1)S(1)}, u32[]{:S(2)}) copy-start(bf16[1,512,192]{1,2,0:T(8,128)(2,1)S(1)} %slice.88) | copy-start | bytes 589828
  36.0 11.4 %copy-start.32 = (bf16[1,512,192]{1,2,0:T(8,128)(2,1)}, bf16[1,512,192]{1,2,0:T(8,128)(2,1)S(1)}, u32[]{:S(2)}) copy-start(bf16[1,512,192]{1,2,0:T(8,128)(2,1)S(1)} %slice.89) | copy-start | bytes 589828
  44.1 3.2 copy-start.34
  47.4 71.8 %copy-start.60 = (f32[768]{0:T(1024)S(1)}, f32[768]{0:T(1024)}, u32[]{:S(2)}) copy-start(f32[768]{0:T(1024)} %param.22) | copy-start | bytes 9220
  47.4 184.2 %all-reduce.12.cloned.1.call-start = ((), (), s32[]{:S(2)}) async-start(), calls=%async_computation.3 | async-start | bytes 3145728 | tf_op jit(solution)/shard_map/psum | solution.py:136
  154.4 7.6 %copy-start.24 = (bf16[192,768]{1,0:T(8,128)(2,1)S(1)}, bf16[192,768]{1,0:T(8,128)(2,1)}, u32[]{:S(2)}) copy-start(bf16[192,768]{1,0:T(8,128)(2,1)} %param.27) | copy-start | bytes 884740
  161.9 69.7 %copy-start.70 = (f32[768]{0:T(1024)S(1)}, f32[768]{0:T(1024)}, u32[]{:S(2)}) copy-start(f32[768]{0:T(1024)} %param.28) | copy-start | bytes 9220
  163.5 149.1 %all-reduce.16.cloned.1.call-start = ((), (), s32[]{:S(2)}) async-start(), calls=%async_computation.5 | async-start | bytes 3145728 | tf_op jit(solution)/shard_map/psum | solution.py:152
  233.3 6.2 copy-start.3
  234.4 5.1 copy-start.53
  234.4 5.1 copy-start.8
  234.4 5.1 copy-start.74
  244.2 113.8 %all-reduce.14.cloned.1.call-start = ((), (), s32[]{:S(2)}) async-start(), calls=%async_computation.4 | async-start | bytes 1572864 | tf_op jit(solution)/shard_map/psum | solution.py:142
  245.3 67.2 %copy-start.54 = (f32[512]{0:T(512)S(1)}, f32[512]{0:T(512)}, u32[]{:S(2)}) copy-start(f32[512]{0:T(512)} %copy-done.53) | copy-start | bytes 6148
  245.3 67.2 %copy-start.59 = (f32[768]{0:T(1024)S(1)}, f32[768]{0:T(1024)}, u32[]{:S(2)}) copy-start(f32[768]{0:T(1024)} %param.29) | copy-start | bytes 9220
  248.3 67.3 %copy-start.52 = (f32[512]{0:T(512)S(1)}, f32[512]{0:T(512)}, u32[]{:S(2)}) copy-start(f32[512]{0:T(512)} %copy-done.51) | copy-start | bytes 6148
  248.3 109.7 %copy-start.69 = (f32[768]{0:T(1024)S(1)}, f32[768]{0:T(1024)}, u32[]{:S(2)}) copy-start(f32[768]{0:T(1024)} %param.34) | copy-start | bytes 9220
  248.4 164.8 %reduce-scatter.3.cloned.1.call-start = ((), (), s32[]{:S(2)}) async-start(), calls=%async_computation.6 | async-start | bytes 1966080 | tf_op jit(solution)/shard_map/reduce_scatter | solution.py:180
  358.1 4.1 copy-start.9
  363.7 10.5 %copy-start.43 = (bf16[512,192]{0,1:T(8,128)(2,1)}, bf16[512,192]{0,1:T(8,128)(2,1)S(1)}, u32[]{:S(2)}) copy-start(bf16[512,192]{0,1:T(8,128)(2,1)S(1)} %convolution_convert_fusion.1) | copy-start | bytes 589828
  363.7 10.5 %slice-start = ((s8[12582912]{0:T(1024)(128)(4,1)}), s8[4194304]{0:T(1024)(128)(4,1)S(1)}, s32[]{:S(2)}) async-start(s8[12582912]{0:T(1024)(128)(4,1)} %bitcast.171), calls=%async_computation.11 | async-start | bytes 8388608
  363.9 11.3 %slice-start.1 = ((s8[12582912]{0:T(1024)(128)(4,1)}), s8[4194304]{0:T(1024)(128)(4,1)S(1)}, s32[]{:S(2)}) async-start(s8[12582912]{0:T(1024)(128)(4,1)} %bitcast.171), calls=%async_computation.12 | async-start | bytes 8388608
  363.9 12.5 %slice-start.2 = ((s8[12582912]{0:T(1024)(128)(4,1)}), s8[4194304]{0:T(1024)(128)(4,1)S(1)}, s32[]{:S(2)}) async-start(s8[12582912]{0:T(1024)(128)(4,1)} %bitcast.171), calls=%async_computation.13 | async-start | bytes 8388608
  376.4 6.0 copy-start.39
  382.4 3.1 copy-start.2
  385.6 59.0 %reduce-scatter.5.cloned.1.call-start = ((), (), s32[]{:S(2)}) async-start(), calls=%async_computation.7 | async-start | bytes 1966080 | tf_op jit(solution)/shard_map/reduce_scatter | solution.py:186
  393.7 125.3 %all-reduce.18.cloned.1.call-start = ((), (), s32[]{:S(2)}) async-start(), calls=%async_computation.8 | async-start | bytes 3145728 | tf_op jit(solution)/shard_map/psum | solution.py:208
  449.7 2.1 copy-start.27
  449.7 2.1 copy-start.41
  449.7 2.1 copy-start.47
  449.7 2.1 copy-start.50
  449.8 3.2 copy-start.31
  449.8 3.2 copy-start.33
  449.8 3.2 copy-start.35
  449.8 136.5 %all-reduce.20.cloned.1.call-start = ((), (), s32[]{:S(2)}) async-start(), calls=%async_computation.9 | async-start | bytes 655360 | tf_op jit(solution)/shard_map/psum | solution.py:237
  451.8 2.0 copy-start.10
  453.8 2.2 copy-start.4
  453.8 2.2 copy-start.78
  453.9 2.2 copy-start.82
  456.1 2.4 copy-start.38
  459.7 61.9 %copy-start.56 = (f32[512]{0:T(512)S(1)}, f32[512]{0:T(512)}, u32[]{:S(2)}) copy-start(f32[512]{0:T(512)} %copy-done.55) | copy-start | bytes 6148
  519.0 2.6 copy-start.7
  519.0 3.4 copy-start.12
  523.5 6.7 copy-start.26
  528.9 3.0 collective-permute-start.2
  534.3 11.8 %copy-start.57 = (f32[512]{0:T(512)S(1)}, f32[512]{0:T(512)}, u32[]{:S(2)}) copy-start(f32[512]{0:T(512)} %copy-done.55) | copy-start | bytes 6148
  534.3 11.8 %copy-start.80 = (f32[768]{0:T(1024)S(1)}, f32[768]{0:T(1024)}, u32[]{:S(2)}) copy-start(f32[768]{0:T(1024)} %param.24) | copy-start | bytes 9220
  536.7 9.5 %copy-start.22 = (bf16[512,3,192]{0,2,1:T(8,128)(2,1)S(1)}, bf16[512,3,192]{0,2,1:T(8,128)(2,1)}, u32[]{:S(2)}) copy-start(bf16[512,3,192]{0,2,1:T(8,128)(2,1)} %copy-done.21) | copy-start | bytes 1769476
  540.0 8.1 %copy-start.17 = (bf16[1,1024,192]{1,2,0:T(8,128)(2,1)}, bf16[1,1024,192]{1,2,0:T(8,128)(2,1)S(1)}, u32[]{:S(2)}) copy-start(bf16[1,1024,192]{1,2,0:T(8,128)(2,1)S(1)} %get-tuple-element.48) | copy-start | bytes 1179652
  540.1 8.0 %collective-permute-start.3 = (bf16[1,1,192]{1,2,0:T(8,128)(2,1)S(1)}, bf16[1,1,192]{1,2,0:T(8,128)(2,1)S(1)}, u32[]{:S(2)}, u32[]{:S(2)}) collective-permute-start(bf16[1,1,192]{1,2,0:T(8,128)(2,1)S(1)} %get-tuple-element.64), channel_id=1, source_target_pairs={{4,0},{8,4},{12,8},{5,1},{9,5},{13,9},{6,2},{10,6},{14,10},{7,3},{... | collective-permute-start | bytes 1160 | tf_op jit(solution)/shard_map/ppermute | solution.py:19
  541.4 6.8 copy-start.45
  541.4 6.7 collective-permute-start.4
  549.4 179.7 %all-reduce.22.cloned.1.call-start = ((), (), s32[]{:S(2)}) async-start(), calls=%async_computation.10 | async-start | bytes 18186240 | tf_op jit(solution)/shard_map/psum | solution.py:240
  732.5 2.9 copy-start.20
  735.5 2.7 copy-start.15
  738.1 2.5 copy-start.14
  738.1 3.9 copy-start.1
  (36 other events, 43.8 us)
Sparse Core Ops, SparseCore 0:
  47.5 71.5 all-reduce.9
  163.6 67.9 all-reduce.11
  244.4 68.1 all-reduce.15
  315.3 42.6 all-reduce.13
  385.7 27.4 reduce-scatter.2
  416.3 28.1 reduce-scatter.4
  449.9 69.0 all-reduce.17
  549.6 36.7 all-reduce.19
  592.7 136.4 all-reduce.21
where the time goes:
time: 757 us; the launch traced here: 749 us
  waiting for transfers between devices  500 us (66%)
  matrix products  76.8 us (10%)
  local copies, waits for them, and re-layouts  58.5 us (8%)
  other arithmetic  43.3 us (6%)
  blocking collectives  43 us (6%)
  between operations  15.3 us (2%)
  starting transfers between devices  11.9 us (2%)
    psum x1, waiting for transfers between devices, on_device(): lax.psum((first_kernel_gradient, first_bias_gradient, second_kernel_gradi...  143 us
    psum x1, waiting for transfers between devices, on_device(): lax.psum(product(attended, output_weight), 'mp')  67.9 us
    psum x1, waiting for transfers between devices, on_device(): stem_pre = lax.psum(product(taps_flat, second_matrix), 'mp') + second_bias  66.7 us
    psum x1, waiting for transfers between devices, on_device(): grad_normed_two = lax.psum(product(grad_expanded, expand_weight.T), 'mp')  64.1 us
    psum x1, waiting for transfers between devices, on_device(): lax.psum(product(grad_packed_flat, project_matrix.T), 'mp')  59.4 us
    psum x1, waiting for transfers between devices, on_device(): lax.psum(product(active, reduce_weight).astype(jnp.bfloat16), 'mp')  42.4 us
    dot_general x19, matrix products, product(): return jnp.dot(left, right, preferred_element_type=jnp.float32)  35.1 us
    reduce_scatter x1, waiting for transfers between devices, on_device(): lax.psum_scatter(values_full.reshape(clips, whole_frames, local_width), '...  31.4 us
  transfers between devices with their start and end apart: 14, of which 11 were waited for; matrix products, arithmetic and copies ran while one was open for 5% of the time, Pallas kernels for 0%

commit v1 on v0

v1 whole, which is shorter than its diff:
```python
import functools
import math

import jax
import jax.numpy as jnp
from jax import lax
from jax.experimental import pallas as pl
from jax.experimental.pallas import tpu as pltpu
from jax.sharding import PartitionSpec as P

HEAD_DIM = 64
BF = jnp.bfloat16
F32 = jnp.float32
VMEM_LIMIT = 48 * 1024 * 1024


def product(left, right, left_dim=1, right_dim=0):
    dims = (((left_dim,), (right_dim,)), ((), ()))
    return lax.dot_general(left, right, dims, preferred_element_type=F32)


def after(value, *others):
    return lax.optimization_barrier((value, *others))[0]


def exact_gelu(value):
    return jax.nn.gelu(value, approximate=False)


def gelu_back(value, grad):
    return jax.vjp(exact_gelu, value)[1](grad)[0]


def layer_norm(value, gain, shift):
    centre = value - jnp.mean(value, axis=-1, keepdims=True)
    spread = jnp.mean(centre * centre, axis=-1, keepdims=True)
    return centre * lax.rsqrt(spread + 1e-05) * gain + shift


def norm_back(value, gain, grad):
    centre = value - jnp.mean(value, axis=-1, keepdims=True)
    spread = jnp.mean(centre * centre, axis=-1, keepdims=True)
    inverse = lax.rsqrt(spread + 1e-05)
    xhat = centre * inverse
    e = grad * gain
    back = (
        e - jnp.mean(e, axis=-1, keepdims=True) - xhat * jnp.mean(e * xhat, axis=-1, keepdims=True)
    ) * inverse
    return back, jnp.sum(grad * xhat, axis=0), jnp.sum(grad, axis=0)


def column_total(value):
    return jnp.sum(value.astype(F32), axis=0)


def sinusoid(start, count, width):
    half = width // 2
    rates = jnp.exp(jnp.arange(half, dtype=F32) * (-math.log(10000.0) / (half - 1)))
    times = (start + jnp.arange(count)).astype(F32)
    angles = times[:, None] * rates[None, :]
    return jnp.concatenate([jnp.sin(angles), jnp.cos(angles)], axis=1)


def turned(size, by):
    return [(i, (i + by) % size) for i in range(size)]


def gather_mp(block):
    size = lax.axis_size("mp")
    return [block] + [lax.ppermute(block, "mp", turned(size, -j)) for j in range(1, size)]


def exchange_mp(blocks):
    size = lax.axis_size("mp")
    got = [lax.ppermute(blocks[j], "mp", turned(size, j)) for j in range(1, size)]
    return [blocks[0]] + got


def row_blocks(value, count):
    rows = value.shape[0] // count
    return [value[j * rows : (j + 1) * rows] for j in range(count)]


def rolled_blocks(value):
    size, z = lax.axis_size("mp"), lax.axis_index("mp")
    rows = value.shape[0] // size
    return [
        lax.dynamic_slice_in_dim(value, lax.rem(z + j, size) * rows, rows, axis=0)
        for j in range(size)
    ]


def natural(blocks):
    size, z = lax.axis_size("mp"), lax.axis_index("mp")
    rows = blocks[0].shape[0]
    twice = jnp.concatenate(blocks + blocks, axis=0)
    return lax.dynamic_slice_in_dim(twice, lax.rem(size - z, size) * rows, rows * size, axis=0)


def total(parts):
    result = parts[0].astype(F32)
    for part in parts[1:]:
        result = result + part.astype(F32)
    return result


def scatter_sum(blocks):
    return total(exchange_mp([blocks[0]] + [block.astype(BF) for block in blocks[1:]]))


def swapped(value, axis, bit):
    size = lax.axis_size(axis)
    return lax.ppermute(value, axis, [(i, i ^ bit) for i in range(size)])


def passed_along(value, by):
    size = lax.axis_size("seq")
    pairs = [(i, i + by) for i in range(size) if 0 <= i + by < size]
    return lax.ppermute(value, "seq", pairs)


def plane_sum(value):
    rows, columns = value.shape
    dp, seq = lax.axis_index("dp"), lax.axis_index("seq")
    dps, seqs = lax.axis_size("dp"), lax.axis_size("seq")
    core = lax.rem(seq, 2)
    half = columns // 2
    mine = lax.dynamic_slice_in_dim(value, core * half, half, axis=1)
    other = lax.dynamic_slice_in_dim(value, (1 - core) * half, half, axis=1)
    mine = mine + swapped(other.astype(BF), "seq", 1).astype(F32)
    quarter = rows // 4
    index = lax.rem(dp, 2) * 2 + lax.div(seq, 2)

    def pairs(d):
        return [
            (p * seqs + s, (p ^ (d >> 1)) * seqs + (s ^ (2 * (d & 1))))
            for p in range(dps)
            for s in range(seqs)
        ]

    def piece(d):
        return lax.dynamic_slice_in_dim(mine, jnp.bitwise_xor(index, d) * quarter, quarter, axis=0)

    result = piece(0)
    got = [lax.ppermute(piece(d).astype(BF), ("dp", "seq"), pairs(d)) for d in (1, 2, 3)]
    result = total([result] + got).astype(BF)
    if dps > 2:
        groups = [[i for i in range(dps) if i % 2 == bit] for bit in range(2)]
        result = lax.psum(result, "dp", axis_index_groups=groups)
    blocks = [result] + [lax.ppermute(result, ("dp", "seq"), pairs(d)) for d in (1, 2, 3)]
    stacked = jnp.stack(blocks)
    ordered = [
        lax.dynamic_index_in_dim(stacked, jnp.bitwise_xor(index, i), 0, keepdims=False)
        for i in range(4)
    ]
    mine = jnp.concatenate(ordered, axis=0)
    other = swapped(mine, "seq", 1)
    return jnp.where(
        core == 0,
        jnp.concatenate([mine, other], axis=1),
        jnp.concatenate([other, mine], axis=1),
    )


def attend_kernel(heads, scale, query_ref, *refs):
    pair_refs, (out_ref, turned_ref, level_ref, held) = refs[:-4], refs[-4:]
    width = heads * HEAD_DIM
    count = pair_refs[0].shape[0]
    outs, levels = [], []
    for head in range(heads):
        cols = slice(head * HEAD_DIM, (head + 1) * HEAD_DIM)
        query = query_ref[:, cols]
        top = None
        for index, pair in enumerate(pair_refs):
            scores = product(pair[:, cols], query, 1, 1) * scale
            held[index * count : (index + 1) * count, :] = scores
            high = jnp.max(scores, axis=0, keepdims=True)
            top = high if top is None else jnp.maximum(top, high)
        weight, out = 0.0, 0.0
        vcols = slice(width + head * HEAD_DIM, width + (head + 1) * HEAD_DIM)
        for index, pair in enumerate(pair_refs):
            soft = jnp.exp(held[index * count : (index + 1) * count, :] - top)
            weight = weight + jnp.sum(soft, axis=0, keepdims=True)
            out = out + product(pair[:, vcols], soft.astype(BF), 0, 0)
        outs.append(out / weight)
        levels.append(top + jnp.log(weight))
    joined = jnp.concatenate(outs, axis=0)
    turned_ref[...] = joined
    out_ref[...] = joined.T.astype(BF)
    level_ref[...] = jnp.concatenate(levels, axis=0)


def attend(query, pairs):
    rows, width = query.shape
    heads = width // HEAD_DIM
    keys = rows * len(pairs)
    return pl.pallas_call(
        functools.partial(attend_kernel, heads, HEAD_DIM ** (-0.5)),
        out_shape=[
            jax.ShapeDtypeStruct((rows, width), BF),
            jax.ShapeDtypeStruct((width, rows), F32),
            jax.ShapeDtypeStruct((heads, rows), F32),
        ],
        scratch_shapes=[pltpu.VMEM((keys, rows), F32)],
        compiler_params=pltpu.CompilerParams(vmem_limit_bytes=VMEM_LIMIT),
        cost_estimate=pl.CostEstimate(
            flops=16 * rows * keys * width,
            bytes_accessed=rows * width * 8 + keys * width * 4,
            transcendentals=rows * keys * heads,
        ),
        name="attend",
    )(query, *pairs)


def attend_back_kernel(heads, scale, query_ref, grad_ref, turned_ref, level_ref, *refs):
    count = (len(refs) - 1) // 2
    pair_refs, query_out, pair_outs = refs[:count], refs[count], refs[count + 1 :]
    width = heads * HEAD_DIM
    grads_turned = grad_ref[...].astype(F32).T
    query_grads = []
    pair_grads = [([], []) for _ in range(count)]
    for head in range(heads):
        cols = slice(head * HEAD_DIM, (head + 1) * HEAD_DIM)
        vcols = slice(width + head * HEAD_DIM, width + (head + 1) * HEAD_DIM)
        query = query_ref[:, cols]
        grad = grad_ref[:, cols]
        level = level_ref[head : head + 1, :]
        delta = jnp.sum(grads_turned[cols, :] * turned_ref[cols, :], axis=0, keepdims=True)
        query_grad = 0.0
        for index in range(count):
            pair = pair_refs[index]
            key = pair[:, cols]
            soft = jnp.exp(product(key, query, 1, 1) * scale - level)
            grad_soft = product(pair[:, vcols], grad, 1, 1)
            low = (soft * (grad_soft - delta)).astype(BF)
            pair_grads[index][0].append(product(low, query) * scale)
            pair_grads[index][1].append(product(soft.astype(BF), grad))
            query_grad = query_grad + product(key, low, 0, 0)
        query_grads.append(query_grad * scale)
    query_out[...] = jnp.concatenate(query_grads, axis=0).T.astype(query_out.dtype)
    for index in range(count):
        joined = jnp.concatenate(pair_grads[index][0] + pair_grads[index][1], axis=1)
        pair_outs[index][...] = joined.astype(pair_outs[index].dtype)


def attend_back(query, grad, turned_out, level, pairs, kinds, name):
    rows, width = query.shape
    heads = width // HEAD_DIM
    keys = rows * len(pairs)
    return pl.pallas_call(
        functools.partial(attend_back_kernel, heads, HEAD_DIM ** (-0.5)),
        out_shape=[jax.ShapeDtypeStruct((rows, width), F32)]
        + [jax.ShapeDtypeStruct((rows, 2 * width), kind) for kind in kinds],
        compiler_params=pltpu.CompilerParams(vmem_limit_bytes=VMEM_LIMIT),
        cost_estimate=pl.CostEstimate(
            flops=40 * rows * keys * width,
            bytes_accessed=rows * width * 8 + keys * width * 8,
            transcendentals=rows * keys * heads,
        ),
        name=name,
    )(query, grad, turned_out, level, *pairs)


def on_device(
    spectrogram,
    first_kernel,
    first_bias,
    second_kernel,
    second_bias,
    attend_gain,
    attend_shift,
    project_weight,
    project_bias,
    output_weight,
    output_bias,
    mixer_gain,
    mixer_shift,
    expand_weight,
    expand_bias,
    reduce_weight,
    reduce_bias,
    cotangent,
):
    _, steps, bands = spectrogram.shape
    frames = steps // 2
    width = first_kernel.shape[2]
    model = second_kernel.shape[2]
    hidden = expand_weight.shape[1]
    mps, seqs = lax.axis_size("mp"), lax.axis_size("seq")
    z, seq = lax.axis_index("mp"), lax.axis_index("seq")
    core = lax.rem(seq, 2)
    rows = frames // mps

    paired = spectrogram.reshape(frames, 2 * bands)
    before = passed_along(paired[-1:], 1)
    following = passed_along(paired[:1], -1)
    ahead = jnp.concatenate([before, paired, following], axis=0)
    window = jnp.concatenate(
        [ahead[:-2, bands:], ahead[1:-1], ahead[2:, :bands]], axis=1
    )
    prior = jnp.concatenate([before, paired[:1, :bands]], axis=1)
    latter = jnp.concatenate([paired[-1:, bands:], following], axis=1)
    first_matrix = first_kernel.reshape(3 * bands, width)
    even_in = jnp.concatenate([window[:, : 3 * bands], latter], axis=0)
    odd_in = jnp.concatenate([prior, window[:, bands:]], axis=0)
    pre_even = product(even_in, first_matrix) + first_bias
    pre_odd = product(odd_in, first_matrix) + first_bias
    inside = jnp.logical_or(jnp.arange(frames + 1) > 0, seq > 0)[:, None]
    hidden_even = exact_gelu(pre_even[:frames]).astype(BF)
    hidden_odd = jnp.where(inside, exact_gelu(pre_odd), 0.0).astype(BF)
    taps = jnp.concatenate([hidden_odd[:frames], hidden_even, hidden_odd[1:]], axis=1)
    second_matrix = second_kernel.reshape(3 * width, model)
    stem_part = product(taps, second_matrix)
    stem_pre = scatter_sum(rolled_blocks(stem_part)) + second_bias
    resid_zero = exact_gelu(stem_pre) + sinusoid(seq * frames + z * rows, rows, model)
    normed_one_blocks = gather_mp(layer_norm(resid_zero, attend_gain, attend_shift).astype(BF))
    normed_one = jnp.concatenate(normed_one_blocks, axis=0)

    project_matrix = project_weight.reshape(model, 3 * width)
    offsets = jnp.concatenate([project_bias[0], jnp.zeros_like(project_bias[0]), project_bias[1]])
    packed = (product(normed_one, project_matrix) + offsets).astype(BF)
    query, pair = packed[:, :width], packed[:, width:]
    pair_far = swapped(pair, "seq", 2)
    pair_core = swapped(pair, "seq", 1)
    pair_far_core = swapped(pair_far, "seq", 1)
    half = model // 2
    weight_half = lax.dynamic_slice_in_dim(output_weight, core * half, half, axis=1)
    weight_half = after(weight_half, pair)
    got = jnp.stack(gather_mp(weight_half)[1:])
    got_other = swapped(got, "seq", 1)
    sides = jnp.where(
        core == 0,
        jnp.concatenate([got, got_other], axis=2),
        jnp.concatenate([got_other, got], axis=2),
    )
    output_whole = jnp.concatenate(
        [output_weight, sides.reshape((mps - 1) * width, model)], axis=0
    )
    attended, attended_turned, level = attend(query, [pair, pair_core, pair_far, pair_far_core])
    heads_got = exchange_mp(row_blocks(attended, mps))
    attended_rows = jnp.concatenate([heads_got[-j % mps] for j in range(mps)], axis=1)
    resid_one = resid_zero + product(attended_rows, output_whole) + output_bias
    normed_two = jnp.concatenate(
        gather_mp(layer_norm(resid_one, mixer_gain, mixer_shift).astype(BF)), axis=0
    )

    own_cotangent = rolled_blocks(cotangent.reshape(frames, model))
    grad_mlp = jnp.concatenate(own_cotangent, axis=0).astype(BF)
    grad_active = product(grad_mlp, reduce_weight, 1, 1)
    expanded = product(normed_two, expand_weight) + expand_bias
    active = exact_gelu(expanded).astype(BF)
    grad_expanded = gelu_back(expanded, grad_active).astype(BF)
    grad_normed_two = scatter_sum(row_blocks(product(grad_expanded, expand_weight, 1, 1), mps))
    back_two, mixer_gain_part, mixer_shift_part = norm_back(resid_one, mixer_gain, grad_normed_two)
    grad_resid_one = own_cotangent[0] + back_two
    grad_attn = grad_resid_one.astype(BF)
    grad_heads = product(grad_attn, output_whole, 1, 1).astype(BF)
    rows_got = exchange_mp([grad_heads[:, j * width : (j + 1) * width] for j in range(mps)])
    grad_attended = jnp.concatenate([rows_got[-j % mps] for j in range(mps)], axis=0)

    active_late = after(active, grad_attended)
    reduce_weight_part = product(active_late, grad_mlp, 0, 0)
    expand_weight_part = product(normed_two, grad_expanded, 0, 0)
    mlp_sums = lax.psum((expand_weight_part.astype(BF), reduce_weight_part.astype(BF)), ("dp", "seq"))
    encoded_part = scatter_sum(row_blocks(product(active_late, reduce_weight), mps))
    encoded_own = (resid_one + encoded_part + reduce_bias).astype(BF)
    encoded = natural(gather_mp(encoded_own)).astype(F32)
    grad_attn_all = gather_mp(after(grad_attn, grad_attended))
    output_weight_part = product(attended, jnp.concatenate(grad_attn_all, axis=0), 0, 0)

    query_grad_far, far, far_core = attend_back(
        query, grad_attended, attended_turned, level, [pair_far, pair_far_core], (F32, BF), "back_far"
    )
    far = far + swapped(far_core, "seq", 1).astype(F32)
    far_got = swapped(far.astype(BF), "seq", 2)
    query_grad_near, near, near_core = attend_back(
        query, grad_attended, attended_turned, level, [pair, pair_core], (F32, BF), "back_near"
    )
    near = near + swapped(near_core, "seq", 1).astype(F32)
    grad_packed = jnp.concatenate(
        [query_grad_far + query_grad_near, near + far_got.astype(F32)], axis=1
    ).astype(BF)
    project_columns = column_total(grad_packed)
    grad_normed_one = scatter_sum(row_blocks(product(grad_packed, project_matrix, 1, 1), mps))
    project_part = product(grad_packed, normed_one, 0, 0)
    late_sums = lax.psum((project_part.astype(BF), output_weight_part.astype(BF)), ("dp", "seq"))
    back_one, attend_gain_part, attend_shift_part = norm_back(
        resid_zero, attend_gain, grad_normed_one
    )
    grad_stem_own = gelu_back(stem_pre, grad_resid_one + back_one).astype(BF)

    small_own = jnp.stack(
        [
            attend_gain_part,
            attend_shift_part,
            mixer_gain_part,
            mixer_shift_part,
            column_total(grad_attn),
            column_total(grad_stem_own),
        ]
    )
    small_own = jnp.concatenate([small_own, jnp.zeros((10, model), F32)], axis=0).astype(BF)
    gathered = gather_mp(jnp.concatenate([grad_stem_own, small_own], axis=0))
    grad_stem = natural([block[:rows] for block in gathered])
    small = natural([block[rows:] for block in gathered]).reshape(mps, 16, model)
    small = jnp.sum(small.astype(F32), axis=0)[:6]
    stem_before = passed_along(grad_stem[-1:], 1)
    stem_following = passed_along(grad_stem[:1], -1)
    second_part = product(taps, grad_stem, 0, 0)
    stem_ahead = jnp.concatenate([stem_before, grad_stem, stem_following], axis=0)
    grad_taps = product(stem_ahead, second_matrix, 1, 1)
    grad_even = grad_taps[1:, width : 2 * width]
    grad_odd = grad_taps[:-1, 2 * width :] + grad_taps[1:, :width]
    grad_pre_even = gelu_back(pre_even, grad_even).astype(BF)
    grad_pre_odd = jnp.where(inside, gelu_back(pre_odd, grad_odd), 0.0).astype(BF)
    first_bias_part = column_total(grad_pre_even[:frames]) + column_total(grad_pre_odd[1:])
    first_part = product(window[:, : 3 * bands], grad_pre_even[:frames], 0, 0) + product(
        window[:, bands:], grad_pre_odd[1:], 0, 0
    )
    back_window = jnp.concatenate(
        [grad_pre_odd[:frames], grad_pre_even[:frames], grad_pre_odd[1:], grad_pre_even[1:]], axis=1
    )
    back_matrix = jnp.transpose(first_kernel[::-1], (0, 2, 1)).reshape(3 * width, bands)
    spectrum_part = jnp.concatenate(
        [
            product(back_window[:, : 3 * width], back_matrix),
            product(back_window[:, width:], back_matrix),
        ],
        axis=1,
    )
    spectrum_own = scatter_sum(rolled_blocks(spectrum_part)).astype(BF)
    spectrogram_gradient = natural(gather_mp(spectrum_own)).astype(F32).reshape(1, steps, bands)

    small_flat = jnp.concatenate(
        [
            small.reshape(-1),
            column_total(cotangent.reshape(frames, model).astype(BF)),
            column_total(grad_expanded),
            project_columns[:width],
            project_columns[2 * width :],
            first_bias_part,
        ]
    )
    first_flat = first_part.reshape(-1, model)
    used = 3 * width + first_flat.shape[0]
    small_rows = -(-small_flat.shape[0] // model)
    padded_rows = -(-(used + small_rows) // 32) * 32
    small_flat = jnp.pad(small_flat, (0, (padded_rows - used) * model - small_flat.shape[0]))
    last = plane_sum(
        jnp.concatenate([second_part, first_flat, small_flat.reshape(-1, model)], axis=0)
    ).astype(F32)
    second_kernel_gradient = last[: 3 * width].reshape(3, width, model)
    first_kernel_gradient = last[3 * width : used].reshape(3, bands, width)
    sums = last[used:].reshape(-1)
    places = {}
    place = 0
    for name, size in (
        ("attend_gain", model),
        ("attend_shift", model),
        ("mixer_gain", model),
        ("mixer_shift", model),
        ("output_bias", model),
        ("second_bias", model),
        ("reduce_bias", model),
        ("expand_bias", hidden),
        ("project_bias", 2 * width),
        ("first_bias", width),
    ):
        places[name] = sums[place : place + size]
        place += size
    return (
        encoded.reshape(1, frames, model),
        spectrogram_gradient,
        first_kernel_gradient,
        places["first_bias"],
        second_kernel_gradient,
        places["second_bias"],
        places["attend_gain"],
        places["attend_shift"],
        late_sums[0].astype(F32).T.reshape(model, 3, width),
        places["project_bias"].reshape(2, width),
        late_sums[1].astype(F32),
        places["output_bias"],
        places["mixer_gain"],
        places["mixer_shift"],
        mlp_sums[0].astype(F32),
        places["expand_bias"],
        mlp_sums[1].astype(F32),
        places["reduce_bias"],
    )


def solution(mesh):
    return jax.shard_map(
        on_device,
        mesh=mesh,
        in_specs=(
            P("dp", "seq", None),
            P(None, None, "mp"),
            P("mp"),
            P(None, "mp", None),
            P(),
            P(),
            P(),
            P(None, None, "mp"),
            P(None, "mp"),
            P("mp", None),
            P(),
            P(),
            P(),
            P(None, "mp"),
            P("mp"),
            P("mp", None),
            P(),
            P("dp", "seq", None),
        ),
        out_specs=(
            P("dp", "seq", None),
            P("dp", "seq", None),
            P(None, None, "mp"),
            P("mp"),
            P(None, "mp", None),
            P(),
            P(),
            P(),
            P(None, None, "mp"),
            P(None, "mp"),
            P("mp", None),
            P(),
            P(),
            P(),
            P(None, "mp"),
            P("mp"),
            P("mp", None),
            P(),
        ),
        check_vma=False,
    )
```

time: 757 us -> 399 us (0.53)
  waiting for transfers between devices: 500 us -> 201 us
  starting transfers between devices: 11.9 us -> 89.8 us
  matrix products: 76.8 us -> 26.4 us
  blocking collectives: 43 us -> 0 us
  local copies, waits for them, and re-layouts: 58.5 us -> 18.8 us
  other arithmetic: 43.3 us -> 25.7 us
  Pallas kernels: 0 us -> 14 us
    psum x7 -> x1, waiting for transfers between devices: 451 us -> 50.4 us  [on_device(): lax.psum((project_part.astype(BF), output_weight_part.astype(BF)), ('dp',...]
    ppermute x5 -> x61, waiting for transfers between devices: 3.76 us -> 151 us  [the longest x21 65.8 us: exchange_mp(): lax.ppermute(blocks[j], 'mp', turned(size, j))]
    ppermute x5 -> x61, starting transfers between devices: 10.9 us -> 89.8 us  [the longest x21 37.4 us: exchange_mp(): lax.ppermute(blocks[j], 'mp', turned(size, j))]
    reduce_scatter x2 -> x0, waiting for transfers between devices: 45.7 us -> none  [the longest x1 31.4 us: on_device(): lax.psum_scatter(values_full.reshape(clips, whole_frames, local_width), '...]
    dot_general x24 -> x21, matrix products: 67.1 us -> 26.4 us  [product(): return lax.dot_general(left, right, dims, preferred_element_type=F32)]
    psum x1 -> x0, blocking collectives: 25.3 us -> none  [on_device(): lax.psum((first_kernel_gradient, first_bias_gradient, second_kernel_gradi...]
    unnamed x179 -> x233, local copies, waits for them, and re-layouts: 25.1 us -> 5.41 us
    slice x9 -> x29, local copies, waits for them, and re-layouts: 27.2 us -> 8.43 us  [the longest x4 1.9 us: on_device(): places[name] = sums[place:place + size]]
  transfers between devices with their start and end apart: 14 -> 62, of which waited for: 11 -> 36; matrix products, arithmetic and copies ran while one was open for 5% -> 7% of each run, Pallas kernels for 0% -> 4%
where the time goes in v1:
time: 399 us; the launch traced here: 393 us
  waiting for transfers between devices  201 us (50%)
  starting transfers between devices  89.8 us (23%)
  matrix products  26.4 us (7%)
  other arithmetic  25.7 us (6%)
  local copies, waits for them, and re-layouts  18.8 us (5%)
  between operations  16.4 us (4%)
  Pallas kernels  14 us (4%)
    ppermute x21, waiting for transfers between devices, exchange_mp(): lax.ppermute(blocks[j], 'mp', turned(size, j))  65.8 us
    ppermute x21, waiting for transfers between devices, gather_mp(): lax.ppermute(block, 'mp', turned(size, -j))  61.6 us
    psum x1, waiting for transfers between devices, on_device(): lax.psum((project_part.astype(BF), output_weight_part.astype(BF)), ('dp',...  50.4 us
    ppermute x21, starting transfers between devices, exchange_mp(): lax.ppermute(blocks[j], 'mp', turned(size, j))  37.4 us
    ppermute x21, starting transfers between devices, gather_mp(): lax.ppermute(block, 'mp', turned(size, -j))  35.3 us
    dot_general x21, matrix products, product(): return lax.dot_general(left, right, dims, preferred_element_type=F32)  26.4 us
    ppermute x3, waiting for transfers between devices, plane_sum(): lax.ppermute(result, ('dp', 'seq'), pairs(d))  10.1 us
    ppermute x9, waiting for transfers between devices, swapped(): return lax.ppermute(value, axis, [(i, i ^ bit) for i in range(size)])  9.52 us
  transfers between devices with their start and end apart: 62, of which 36 were waited for; matrix products, arithmetic and copies ran while one was open for 7% of the time, Pallas kernels for 4%

profile of v1, /device:TPU:0, one launch (start us, length us, event | category | flops | bytes accessed | tf_op | source)
XLA Modules:
  0.0 392.5 jit_solution(6988294996765718103)
XLA Ops:
  9.8 3.0 collective-permute-start
  15.8 2.3 select_convert_fusion.1
  19.8 3.1 collective-permute-start.2
  22.9 2.1 collective-permute-start.4
  26.7 3.7 collective-permute-done.2
  30.4 4.3 %collective-permute-done.4 = bf16[128,768]{1,0:T(8,128)(2,1)S(1)} collective-permute-done((bf16[128,768]{1,0:T(8,128)(2,1)S(1)}, bf16[128,768]{1,0:T(8,128)(2,1)S(1)}, u32[]{:S(2)}, u32[]{:S(2)}) %collective-permute-start.4) | collective-permute-done | bytes 196640 | tf_op jit(solution)/shard_map/ppermute | solution.py:75
  34.8 8.5 %collective-permute-done.3 = bf16[128,768]{1,0:T(8,128)(2,1)S(1)} collective-permute-done((bf16[128,768]{1,0:T(8,128)(2,1)S(1)}, bf16[128,768]{1,0:T(8,128)(2,1)S(1)}, u32[]{:S(2)}, u32[]{:S(2)}) %collective-permute-start.3) | collective-permute-done | bytes 196640 | tf_op jit(solution)/shard_map/ppermute | solution.py:75
  45.4 2.3 collective-permute-start.6
  47.6 1.6 collective-permute-start.5
  49.3 5.7 %collective-permute-done.7 = bf16[128,768]{1,0:T(8,128)(2,1)S(1)} collective-permute-done((bf16[128,768]{1,0:T(8,128)(2,1)S(1)}, bf16[128,768]{1,0:T(8,128)(2,1)S(1)}, u32[]{:S(2)}, u32[]{:S(2)}) %collective-permute-start.7) | collective-permute-done | bytes 196640 | tf_op jit(solution)/shard_map/ppermute | solution.py:70
  55.0 7.5 %collective-permute-done.6 = bf16[128,768]{1,0:T(8,128)(2,1)S(1)} collective-permute-done((bf16[128,768]{1,0:T(8,128)(2,1)S(1)}, bf16[128,768]{1,0:T(8,128)(2,1)S(1)}, u32[]{:S(2)}, u32[]{:S(2)}) %collective-permute-start.6) | collective-permute-done | bytes 196640 | tf_op jit(solution)/shard_map/ppermute | solution.py:70
  63.8 9.3 %collective-permute-done.9.refs_2_.refs_0_ = bf16[512,384]{1,0:T(8,128)(2,1)S(1)} collective-permute-done((bf16[512,384]{1,0:T(8,128)(2,1)S(1)}, bf16[512,384]{1,0:T(8,128)(2,1)S(1)}, u32[]{:S(2)}, u32[]{:S(2)}) %collective-permute-start.9) | collective-permute-done | bytes 393248 | tf_op jit(solution)/shard_map/ppermute | solution.py:113
  73.8 4.8 %collective-permute-start.16 = (bf16[192,384]{1,0:T(8,128)(2,1)}, bf16[192,384]{1,0:T(8,128)(2,1)S(1)}, u32[]{:S(2)}, u32[]{:S(2)}) collective-permute-start(bf16[192,384]{1,0:T(8,128)(2,1)} %constant_dynamic-slice_fusion.4), channel_id=1, source_target_pairs={{0,1},{1,2},{2,3},{3,0},{4,5},{5,6},{6,7},{7,4},{8,9},{9,10},{10,1... | collective-permute-start | bytes 442376 | tf_op jit(solution)/shard_map/ppermute | solution.py:70
  78.6 2.5 collective-permute-start.14
  83.1 5.6 %collective-permute-done.15 = bf16[192,384]{1,0:T(8,128)(2,1)} collective-permute-done((bf16[192,384]{1,0:T(8,128)(2,1)}, bf16[192,384]{1,0:T(8,128)(2,1)}, u32[]{:S(2)}, u32[]{:S(2)}) %collective-permute-start.15) | collective-permute-done | bytes 147488 | tf_op jit(solution)/shard_map/ppermute | solution.py:70
  90.2 5.6 %attend.1 = (bf16[512,192]{1,0:T(8,128)(2,1)S(1)}, f32[192,512]{1,0:T(8,128)S(1)}, f32[3,512]{1,0:T(4,128)S(1)}) custom-call(bf16[512,192]{1,0:T(8,128)(2,1)S(1)} %slice.338.query_ref, bf16[512,384]{1,0:T(8,128)(2,1)S(1)} %slice.339.refs_0_, bf16[512,384]{1,0:T(8,128)(2,1)S(1)} %collective-permute-done.8.refs_1_, ...), custom_call_target="tpu_custom_call" | custom-call | flops 3221225472 | bytes 2359296 | tf_op jit(solution)/shard_map/attend/pallas_call | solution.py:197
  95.9 3.4 collective-permute-start.13
  99.3 3.4 collective-permute-start.12
  102.9 2.3 collective-permute-done.13
  105.2 2.6 collective-permute-done.12
  113.3 5.7 %collective-permute-done.20 = bf16[128,768]{1,0:T(8,128)(2,1)S(1)} collective-permute-done((bf16[128,768]{1,0:T(8,128)(2,1)S(1)}, bf16[128,768]{1,0:T(8,128)(2,1)S(1)}, u32[]{:S(2)}, u32[]{:S(2)}) %collective-permute-start.20) | collective-permute-done | bytes 196640 | tf_op jit(solution)/shard_map/ppermute | solution.py:70
  119.1 7.0 %collective-permute-done.19 = bf16[128,768]{1,0:T(8,128)(2,1)S(1)} collective-permute-done((bf16[128,768]{1,0:T(8,128)(2,1)S(1)}, bf16[128,768]{1,0:T(8,128)(2,1)S(1)}, u32[]{:S(2)}, u32[]{:S(2)}) %collective-permute-start.19) | collective-permute-done | bytes 196640 | tf_op jit(solution)/shard_map/ppermute | solution.py:70
  126.0 5.3 %multiply_convert_fusion = (bf16[512,768]{1,0:T(8,128)(2,1)}, f32[512,768]{1,0:T(8,128)S(1)}, f32[512,768]{1,0:T(8,128)S(1)}) fusion(f32[768]{0:T(1024)S(1)} %copy-done.104, bf16[768,768]{1,0:T(8,128)(2,1)S(1)} %copy-done, bf16[128,768]{1,0:T(8,128)(2,1)S(1)} %collective-permute-done.20, bf16[128,768]{1,0:T(8,128)(2,1)S(1)} %collective-permute-done.19, ...), kind=kOutput, calls=%fused_computation.6 | convolution fusion | flops 633077760 | bytes 5901312 | tf_op jit(solution)/shard_map/dot_general | solution.py:19
  131.4 1.8 convert_reduce_fusion
  133.2 2.0 fusion.167
  135.8 4.7 %collective-permute-start.21 = (bf16[128,768]{1,0:T(8,128)(2,1)}, bf16[128,768]{1,0:T(8,128)(2,1)}, u32[]{:S(2)}, u32[]{:S(2)}) collective-permute-start(bf16[128,768]{1,0:T(8,128)(2,1)} %get-tuple-element.117), channel_id=1, source_target_pairs={{0,1},{1,2},{2,3},{3,0},{4,5},{5,6},{6,7},{7,4},{8,9},{9,10},{10,1... | collective-permute-start | bytes 589832 | tf_op jit(solution)/shard_map/ppermute | solution.py:75
  143.1 2.1 convert_reduce_fusion.1
  146.8 3.5 collective-permute-done.23
  150.3 8.0 %collective-permute-done.22 = bf16[128,768]{1,0:T(8,128)(2,1)} collective-permute-done((bf16[128,768]{1,0:T(8,128)(2,1)S(1)}, bf16[128,768]{1,0:T(8,128)(2,1)}, u32[]{:S(2)}, u32[]{:S(2)}) %collective-permute-start.22) | collective-permute-done | bytes 196640 | tf_op jit(solution)/shard_map/ppermute | solution.py:75
  158.3 1.7 multiply_reduce_fusion
  162.0 3.2 collective-permute-start.25
  165.9 1.8 convolution_convert_fusion.1
  168.7 1.8 collective-permute-done.25
  172.0 1.7 collective-permute-start.59
  173.7 1.8 convolution_convert_fusion
  177.8 2.5 collective-permute-start.29
  180.2 4.2 %back_near.1 = (f32[512,192]{1,0:T(8,128)S(1)}, f32[512,384]{1,0:T(8,128)S(1)}, bf16[512,384]{1,0:T(8,128)(2,1)S(1)}) custom-call(bf16[512,192]{1,0:T(8,128)(2,1)S(1)} %slice.338.query_ref, bf16[512,192]{1,0:T(8,128)(2,1)S(1)} %pad_maximum_fusion.12.grad_ref, f32[192,512]{1,0:T(8,128)S(1)} %copy-done.3, f32[3,512]{1,0:T(4,128)S(1)} %get-tuple-element.34.level_ref, ...), custom_call_target="tpu_custom_call" | custom-call | flops 4026531840 | bytes 2359296 | tf_op jit(solution)/shard_map/back_near/pallas_call | solution.py:250
  184.4 4.2 %back_far.1 = (f32[512,192]{1,0:T(8,128)S(1)}, f32[512,384]{1,0:T(8,128)S(1)}, bf16[512,384]{1,0:T(8,128)(2,1)S(1)}) custom-call(bf16[512,192]{1,0:T(8,128)(2,1)S(1)} %slice.338.query_ref, bf16[512,192]{1,0:T(8,128)(2,1)S(1)} %pad_maximum_fusion.12.grad_ref, f32[192,512]{1,0:T(8,128)S(1)} %copy-done.3, f32[3,512]{1,0:T(4,128)S(1)} %get-tuple-element.34.level_ref, ...), custom_call_target="tpu_custom_call" | custom-call | flops 4026531840 | bytes 2359296 | tf_op jit(solution)/shard_map/back_far/pallas_call | solution.py:250
  188.7 2.4 collective-permute-start.58
  191.1 11.9 %collective-permute-done.28 = bf16[128,768]{1,0:T(8,128)(2,1)S(1)} collective-permute-done((bf16[128,768]{1,0:T(8,128)(2,1)S(1)}, bf16[128,768]{1,0:T(8,128)(2,1)S(1)}, u32[]{:S(2)}, u32[]{:S(2)}) %collective-permute-start.28) | collective-permute-done | bytes 196640 | tf_op jit(solution)/shard_map/ppermute | solution.py:75
  203.1 2.7 collective-permute-start.32
  205.8 3.4 collective-permute-start.31
  211.0 8.0 %collective-permute-done.30 = bf16[128,768]{1,0:T(8,128)(2,1)S(1)} collective-permute-done((bf16[128,768]{1,0:T(8,128)(2,1)S(1)}, bf16[128,768]{1,0:T(8,128)(2,1)S(1)}, u32[]{:S(2)}, u32[]{:S(2)}) %collective-permute-start.30) | collective-permute-done | bytes 196640 | tf_op jit(solution)/shard_map/ppermute | solution.py:70
  219.1 3.7 collective-permute-done.31
  224.9 4.8 %collective-permute-start.36 = (bf16[128,768]{1,0:T(8,128)(2,1)S(1)}, bf16[128,768]{1,0:T(8,128)(2,1)S(1)}, u32[]{:S(2)}, u32[]{:S(2)}) collective-permute-start(bf16[128,768]{1,0:T(8,128)(2,1)S(1)} %get-tuple-element.111), channel_id=1, source_target_pairs={{0,1},{1,2},{2,3},{3,0},{4,5},{5,6},{6,7},{7,4},{8,9},{9,10},{10,1... | collective-permute-start | bytes 589832 | tf_op jit(solution)/shard_map/ppermute | solution.py:75
  229.7 1.6 collective-permute-start.37
  231.6 3.3 collective-permute-done.36
  235.0 4.3 %collective-permute-done.38 = bf16[128,768]{1,0:T(8,128)(2,1)S(1)} collective-permute-done((bf16[128,768]{1,0:T(8,128)(2,1)S(1)}, bf16[128,768]{1,0:T(8,128)(2,1)S(1)}, u32[]{:S(2)}, u32[]{:S(2)}) %collective-permute-start.38) | collective-permute-done | bytes 196640 | tf_op jit(solution)/shard_map/ppermute | solution.py:75
  239.2 7.0 %collective-permute-done.37 = bf16[128,768]{1,0:T(8,128)(2,1)S(1)} collective-permute-done((bf16[128,768]{1,0:T(8,128)(2,1)S(1)}, bf16[128,768]{1,0:T(8,128)(2,1)S(1)}, u32[]{:S(2)}, u32[]{:S(2)}) %collective-permute-start.37) | collective-permute-done | bytes 196640 | tf_op jit(solution)/shard_map/ppermute | solution.py:75
  246.6 2.2 fusion.146
  249.1 3.7 collective-permute-start.39
  253.5 8.6 %collective-permute-done.39 = bf16[144,768]{1,0:T(8,128)(2,1)S(1)} collective-permute-done((bf16[144,768]{1,0:T(8,128)(2,1)S(1)}, bf16[144,768]{1,0:T(8,128)(2,1)S(1)}, u32[]{:S(2)}, u32[]{:S(2)}) %collective-permute-start.39) | collective-permute-done | bytes 221216 | tf_op jit(solution)/shard_map/ppermute | solution.py:70
  262.1 8.4 %collective-permute-done.40 = bf16[144,768]{1,0:T(8,128)(2,1)S(1)} collective-permute-done((bf16[144,768]{1,0:T(8,128)(2,1)S(1)}, bf16[144,768]{1,0:T(8,128)(2,1)S(1)}, u32[]{:S(2)}, u32[]{:S(2)}) %collective-permute-start.40) | collective-permute-done | bytes 221216 | tf_op jit(solution)/shard_map/ppermute | solution.py:70
  275.8 2.3 fusion.9
  282.9 2.4 collective-permute-start.50
  285.9 3.2 collective-permute-start.45
  293.4 3.1 collective-permute-start.47
  296.8 3.3 collective-permute-start.53
  300.3 1.8 convolution_convert_fusion.2
  309.4 6.4 %collective-permute-done.56 = bf16[168,384]{1,0:T(8,128)(2,1)S(1)} collective-permute-done((bf16[168,384]{1,0:T(8,128)(2,1)S(1)}, bf16[168,384]{1,0:T(8,128)(2,1)S(1)}, u32[]{:S(2)}, u32[]{:S(2)}) %collective-permute-start.56) | collective-permute-done | bytes 129056 | tf_op jit(solution)/shard_map/ppermute | solution.py:150
  315.8 3.7 collective-permute-done.55
  327.4 50.4 %all-reduce.4.cloned.1.call-done = (bf16[768,3,192]{0,2,1:T(8,128)(2,1)}, bf16[192,768]{1,0:T(8,128)(2,1)}, bf16[768,768]{1,0:T(8,128)(2,1)}, bf16[768,768]{1,0:T(8,128)(2,1)}) async-done(((bf16[768,3,192]{0,2,1:T(8,128)(2,1)}, bf16[192,768]{1,0:T(8,128)(2,1)}, bf16[768,768]{1,0:T(8,128)(2,1)}, bf16[768,768]{1,0:T(8,128)(2,1)}), (bf16[768,3,192]{0,2,1:T(8,128)(2,1)}, bf16[192,768]{1,0:T(8,128)(2,1)}, ...) | async-done | bytes 3538960 | tf_op jit(solution)/shard_map/psum | solution.py:386
  377.8 1.9 convert_element_type.286
  379.7 2.5 reshape.200
  (434 shorter events, 72.9 us)
Async XLA Ops:
  7.2 118.8 %copy-start = (bf16[768,768]{1,0:T(8,128)(2,1)S(1)}, bf16[768,768]{1,0:T(8,128)(2,1)}, u32[]{:S(2)}) copy-start(bf16[768,768]{1,0:T(8,128)(2,1)} %param.31) | copy-start | bytes 3538948
  7.2 370.6 %all-reduce.4.cloned.1.call-start = ((), (), s32[]{:S(2)}) async-start(), calls=%async_computation | async-start | bytes 7077888 | tf_op jit(solution)/shard_map/psum | solution.py:386
  8.4 5.9 %collective-permute-start.1 = (bf16[1,160]{1,0:T(2,128)(2,1)S(1)}, bf16[1,160]{1,0:T(2,128)(2,1)S(1)}, u32[]{:S(2)}, u32[]{:S(2)}) collective-permute-start(bf16[1,160]{1,0:T(2,128)(2,1)S(1)} %slice.262), channel_id=1, source_target_pairs={{4,0},{8,4},{12,8},{5,1},{9,5},{13,9},{6,2},{10,6},{14,10},{7,3},{... | collective-permute-start | bytes 968 | tf_op jit(solution)/shard_map/ppermute | solution.py:119
  9.8 4.5 %collective-permute-start = (bf16[1,160]{1,0:T(2,128)(2,1)S(1)}, bf16[1,160]{1,0:T(2,128)(2,1)S(1)}, u32[]{:S(2)}, u32[]{:S(2)}) collective-permute-start(bf16[1,160]{1,0:T(2,128)(2,1)S(1)} %slice.259), channel_id=1, source_target_pairs={{0,4},{4,8},{8,12},{1,5},{5,9},{9,13},{2,6},{6,10},{10,14},{3,7},{... | collective-permute-start | bytes 968 | tf_op jit(solution)/shard_map/ppermute | solution.py:119
  19.8 10.6 %collective-permute-start.2 = (bf16[128,768]{1,0:T(8,128)(2,1)S(1)}, bf16[128,768]{1,0:T(8,128)(2,1)S(1)}, u32[]{:S(2)}, u32[]{:S(2)}) collective-permute-start(bf16[128,768]{1,0:T(8,128)(2,1)S(1)} %get-tuple-element.103), channel_id=1, source_target_pairs={{0,1},{1,2},{2,3},{3,0},{4,5},{5,6},{6,7},{7,4},{8,9},{9,10},{10,1... | collective-permute-start | bytes 589832 | tf_op jit(solution)/shard_map/ppermute | solution.py:75
  22.9 11.9 %collective-permute-start.4 = (bf16[128,768]{1,0:T(8,128)(2,1)S(1)}, bf16[128,768]{1,0:T(8,128)(2,1)S(1)}, u32[]{:S(2)}, u32[]{:S(2)}) collective-permute-start(bf16[128,768]{1,0:T(8,128)(2,1)S(1)} %get-tuple-element.104), channel_id=1, source_target_pairs={{0,3},{1,0},{2,1},{3,2},{4,7},{5,4},{6,5},{7,6},{8,11},{9,8},{10,9... | collective-permute-start | bytes 589832 | tf_op jit(solution)/shard_map/ppermute | solution.py:75
  25.0 18.3 %collective-permute-start.3 = (bf16[128,768]{1,0:T(8,128)(2,1)S(1)}, bf16[128,768]{1,0:T(8,128)(2,1)S(1)}, u32[]{:S(2)}, u32[]{:S(2)}) collective-permute-start(bf16[128,768]{1,0:T(8,128)(2,1)S(1)} %get-tuple-element.105), channel_id=1, source_target_pairs={{0,2},{1,3},{2,0},{3,1},{4,6},{5,7},{6,4},{7,5},{8,10},{9,11},{10,... | collective-permute-start | bytes 589832 | tf_op jit(solution)/shard_map/ppermute | solution.py:75
  45.3 9.8 %collective-permute-start.7 = (bf16[128,768]{1,0:T(8,128)(2,1)S(1)}, bf16[128,768]{1,0:T(8,128)(2,1)S(1)}, u32[]{:S(2)}, u32[]{:S(2)}) collective-permute-start(bf16[128,768]{1,0:T(8,128)(2,1)S(1)} %add_convert_fusion.6), channel_id=1, source_target_pairs={{0,1},{1,2},{2,3},{3,0},{4,5},{5,6},{6,7},{7,4},{8,9},{9,10},{10,1... | collective-permute-start | bytes 589832 | tf_op jit(solution)/shard_map/ppermute | solution.py:70
  45.4 17.2 %collective-permute-start.6 = (bf16[128,768]{1,0:T(8,128)(2,1)S(1)}, bf16[128,768]{1,0:T(8,128)(2,1)S(1)}, u32[]{:S(2)}, u32[]{:S(2)}) collective-permute-start(bf16[128,768]{1,0:T(8,128)(2,1)S(1)} %add_convert_fusion.6), channel_id=1, source_target_pairs={{0,2},{1,3},{2,0},{3,1},{4,6},{5,7},{6,4},{7,5},{8,10},{9,11},{10,... | collective-permute-start | bytes 589832 | tf_op jit(solution)/shard_map/ppermute | solution.py:70
  47.6 14.9 %collective-permute-start.5 = (bf16[128,768]{1,0:T(8,128)(2,1)S(1)}, bf16[128,768]{1,0:T(8,128)(2,1)S(1)}, u32[]{:S(2)}, u32[]{:S(2)}) collective-permute-start(bf16[128,768]{1,0:T(8,128)(2,1)S(1)} %add_convert_fusion.6), channel_id=1, source_target_pairs={{0,3},{1,0},{2,1},{3,2},{4,7},{5,4},{6,5},{7,6},{8,11},{9,8},{10,9... | collective-permute-start | bytes 589832 | tf_op jit(solution)/shard_map/ppermute | solution.py:70
  63.7 9.5 %collective-permute-start.9 = (bf16[512,384]{1,0:T(8,128)(2,1)S(1)}, bf16[512,384]{1,0:T(8,128)(2,1)S(1)}, u32[]{:S(2)}, u32[]{:S(2)}) collective-permute-start(bf16[512,384]{1,0:T(8,128)(2,1)S(1)} %slice.339.refs_0_), channel_id=1, source_target_pairs={{0,8},{4,12},{8,0},{12,4},{1,9},{5,13},{9,1},{13,5},{2,10},{6,14},... | collective-permute-start | bytes 1179656 | tf_op jit(solution)/shard_map/ppermute | solution.py:113
  63.8 26.4 %collective-permute-start.8 = (bf16[512,384]{1,0:T(8,128)(2,1)S(1)}, bf16[512,384]{1,0:T(8,128)(2,1)S(1)}, u32[]{:S(2)}, u32[]{:S(2)}) collective-permute-start(bf16[512,384]{1,0:T(8,128)(2,1)S(1)} %slice.339.refs_0_), channel_id=1, source_target_pairs={{0,4},{4,0},{8,12},{12,8},{1,5},{5,1},{9,13},{13,9},{2,6},{6,2},{1... | collective-permute-start | bytes 1179656 | tf_op jit(solution)/shard_map/ppermute | solution.py:113
  73.1 17.0 %collective-permute-start.10 = (bf16[512,384]{1,0:T(8,128)(2,1)S(1)}, bf16[512,384]{1,0:T(8,128)(2,1)S(1)}, u32[]{:S(2)}, u32[]{:S(2)}) collective-permute-start(bf16[512,384]{1,0:T(8,128)(2,1)S(1)} %collective-permute-done.9.refs_2_.refs_0_), channel_id=1, source_target_pairs={{0,4},{4,0},{8,12},{12,8},{1,5},{5,1},{9,13},{13,9},{2,6},{6,2},{1... | collective-permute-start | bytes 1179656 | tf_op jit(solution)/shard_map/ppermute | solution.py:113
  73.8 9.2 %collective-permute-start.16 = (bf16[192,384]{1,0:T(8,128)(2,1)}, bf16[192,384]{1,0:T(8,128)(2,1)S(1)}, u32[]{:S(2)}, u32[]{:S(2)}) collective-permute-start(bf16[192,384]{1,0:T(8,128)(2,1)} %constant_dynamic-slice_fusion.4), channel_id=1, source_target_pairs={{0,1},{1,2},{2,3},{3,0},{4,5},{5,6},{6,7},{7,4},{8,9},{9,10},{10,1... | collective-permute-start | bytes 442376 | tf_op jit(solution)/shard_map/ppermute | solution.py:70
  78.6 10.1 %collective-permute-start.15 = (bf16[192,384]{1,0:T(8,128)(2,1)}, bf16[192,384]{1,0:T(8,128)(2,1)}, u32[]{:S(2)}, u32[]{:S(2)}) collective-permute-start(bf16[192,384]{1,0:T(8,128)(2,1)} %constant_dynamic-slice_fusion.4), channel_id=1, source_target_pairs={{0,2},{1,3},{2,0},{3,1},{4,6},{5,7},{6,4},{7,5},{8,10},{9,11},{10,... | collective-permute-start | bytes 442376 | tf_op jit(solution)/shard_map/ppermute | solution.py:70
  78.6 10.4 %collective-permute-start.14 = (bf16[192,384]{1,0:T(8,128)(2,1)}, bf16[192,384]{1,0:T(8,128)(2,1)}, u32[]{:S(2)}, u32[]{:S(2)}) collective-permute-start(bf16[192,384]{1,0:T(8,128)(2,1)} %constant_dynamic-slice_fusion.4), channel_id=1, source_target_pairs={{0,3},{1,0},{2,1},{3,2},{4,7},{5,4},{6,5},{7,6},{8,11},{9,8},{10,9... | collective-permute-start | bytes 442376 | tf_op jit(solution)/shard_map/ppermute | solution.py:70
  90.1 12.7 %collective-permute-start.17 = (bf16[3,192,384]{2,1,0:T(8,128)(2,1)S(1)}, bf16[3,192,384]{2,1,0:T(8,128)(2,1)S(1)}, u32[]{:S(2)}, u32[]{:S(2)}) collective-permute-start(bf16[3,192,384]{2,1,0:T(8,128)(2,1)S(1)} %pad_maximum_fusion.11), channel_id=1, source_target_pairs={{0,4},{4,0},{8,12},{12,8},{1,5},{5,1},{9,13},{13,9},{2,6},{6,2},{1... | collective-permute-start | bytes 1327112 | tf_op jit(solution)/shard_map/ppermute | solution.py:113
  95.9 9.3 %collective-permute-start.13 = (bf16[128,192]{1,0:T(8,128)(2,1)S(1)}, bf16[128,192]{1,0:T(8,128)(2,1)S(1)}, u32[]{:S(2)}, u32[]{:S(2)}) collective-permute-start(bf16[128,192]{1,0:T(8,128)(2,1)S(1)} %get-tuple-element.128), channel_id=1, source_target_pairs={{0,1},{1,2},{2,3},{3,0},{4,5},{5,6},{6,7},{7,4},{8,9},{9,10},{10,1... | collective-permute-start | bytes 147464 | tf_op jit(solution)/shard_map/ppermute | solution.py:75
  99.3 8.5 %collective-permute-start.12 = (bf16[128,192]{1,0:T(8,128)(2,1)S(1)}, bf16[128,192]{1,0:T(8,128)(2,1)S(1)}, u32[]{:S(2)}, u32[]{:S(2)}) collective-permute-start(bf16[128,192]{1,0:T(8,128)(2,1)S(1)} %get-tuple-element.129), channel_id=1, source_target_pairs={{0,2},{1,3},{2,0},{3,1},{4,6},{5,7},{6,4},{7,5},{8,10},{9,11},{10,... | collective-permute-start | bytes 147464 | tf_op jit(solution)/shard_map/ppermute | solution.py:75
  102.7 5.5 %collective-permute-start.11 = (bf16[128,192]{1,0:T(8,128)(2,1)S(1)}, bf16[128,192]{1,0:T(8,128)(2,1)S(1)}, u32[]{:S(2)}, u32[]{:S(2)}) collective-permute-start(bf16[128,192]{1,0:T(8,128)(2,1)S(1)} %get-tuple-element.130), channel_id=1, source_target_pairs={{0,3},{1,0},{2,1},{3,2},{4,7},{5,4},{6,5},{7,6},{8,11},{9,8},{10,9... | collective-permute-start | bytes 147464 | tf_op jit(solution)/shard_map/ppermute | solution.py:75
  109.2 9.8 %collective-permute-start.20 = (bf16[128,768]{1,0:T(8,128)(2,1)S(1)}, bf16[128,768]{1,0:T(8,128)(2,1)S(1)}, u32[]{:S(2)}, u32[]{:S(2)}) collective-permute-start(bf16[128,768]{1,0:T(8,128)(2,1)S(1)} %add_convert_fusion.5), channel_id=1, source_target_pairs={{0,1},{1,2},{2,3},{3,0},{4,5},{5,6},{6,7},{7,4},{8,9},{9,10},{10,1... | collective-permute-start | bytes 589832 | tf_op jit(solution)/shard_map/ppermute | solution.py:70
  110.7 15.3 %collective-permute-start.19 = (bf16[128,768]{1,0:T(8,128)(2,1)S(1)}, bf16[128,768]{1,0:T(8,128)(2,1)S(1)}, u32[]{:S(2)}, u32[]{:S(2)}) collective-permute-start(bf16[128,768]{1,0:T(8,128)(2,1)S(1)} %add_convert_fusion.5), channel_id=1, source_target_pairs={{0,2},{1,3},{2,0},{3,1},{4,6},{5,7},{6,4},{7,5},{8,10},{9,11},{10,... | collective-permute-start | bytes 589832 | tf_op jit(solution)/shard_map/ppermute | solution.py:70
  112.0 14.0 %collective-permute-start.18 = (bf16[128,768]{1,0:T(8,128)(2,1)S(1)}, bf16[128,768]{1,0:T(8,128)(2,1)S(1)}, u32[]{:S(2)}, u32[]{:S(2)}) collective-permute-start(bf16[128,768]{1,0:T(8,128)(2,1)S(1)} %add_convert_fusion.5), channel_id=1, source_target_pairs={{0,3},{1,0},{2,1},{3,2},{4,7},{5,4},{6,5},{7,6},{8,11},{9,8},{10,9... | collective-permute-start | bytes 589832 | tf_op jit(solution)/shard_map/ppermute | solution.py:70
  135.8 11.0 %collective-permute-start.21 = (bf16[128,768]{1,0:T(8,128)(2,1)}, bf16[128,768]{1,0:T(8,128)(2,1)}, u32[]{:S(2)}, u32[]{:S(2)}) collective-permute-start(bf16[128,768]{1,0:T(8,128)(2,1)} %get-tuple-element.117), channel_id=1, source_target_pairs={{0,1},{1,2},{2,3},{3,0},{4,5},{5,6},{6,7},{7,4},{8,9},{9,10},{10,1... | collective-permute-start | bytes 589832 | tf_op jit(solution)/shard_map/ppermute | solution.py:75
  140.5 9.8 %collective-permute-start.23 = (bf16[128,768]{1,0:T(8,128)(2,1)S(1)}, bf16[128,768]{1,0:T(8,128)(2,1)}, u32[]{:S(2)}, u32[]{:S(2)}) collective-permute-start(bf16[128,768]{1,0:T(8,128)(2,1)S(1)} %get-tuple-element.118), channel_id=1, source_target_pairs={{0,3},{1,0},{2,1},{3,2},{4,7},{5,4},{6,5},{7,6},{8,11},{9,8},{10,9... | collective-permute-start | bytes 589832 | tf_op jit(solution)/shard_map/ppermute | solution.py:75
  140.9 17.4 %collective-permute-start.22 = (bf16[128,768]{1,0:T(8,128)(2,1)S(1)}, bf16[128,768]{1,0:T(8,128)(2,1)}, u32[]{:S(2)}, u32[]{:S(2)}) collective-permute-start(bf16[128,768]{1,0:T(8,128)(2,1)S(1)} %get-tuple-element.119), channel_id=1, source_target_pairs={{0,2},{1,3},{2,0},{3,1},{4,6},{5,7},{6,4},{7,5},{8,10},{9,11},{10,... | collective-permute-start | bytes 589832 | tf_op jit(solution)/shard_map/ppermute | solution.py:75
  161.9 6.8 %collective-permute-start.26 = (bf16[128,192]{1,0:T(8,128)(2,1)S(1)}, bf16[128,192]{1,0:T(8,128)(2,1)S(1)}, u32[]{:S(2)}, u32[]{:S(2)}) collective-permute-start(bf16[128,192]{1,0:T(8,128)(2,1)S(1)} %get-tuple-element.142), channel_id=1, source_target_pairs={{0,1},{1,2},{2,3},{3,0},{4,5},{5,6},{6,7},{7,4},{8,9},{9,10},{10,1... | collective-permute-start | bytes 147464 | tf_op jit(solution)/shard_map/ppermute | solution.py:75
  162.0 8.5 %collective-permute-start.25 = (bf16[128,192]{1,0:T(8,128)(2,1)S(1)}, bf16[128,192]{1,0:T(8,128)(2,1)S(1)}, u32[]{:S(2)}, u32[]{:S(2)}) collective-permute-start(bf16[128,192]{1,0:T(8,128)(2,1)S(1)} %get-tuple-element.143), channel_id=1, source_target_pairs={{0,2},{1,3},{2,0},{3,1},{4,6},{5,7},{6,4},{7,5},{8,10},{9,11},{10,... | collective-permute-start | bytes 147464 | tf_op jit(solution)/shard_map/ppermute | solution.py:75
  165.2 5.3 %collective-permute-start.24 = (bf16[128,192]{1,0:T(8,128)(2,1)S(1)}, bf16[128,192]{1,0:T(8,128)(2,1)S(1)}, u32[]{:S(2)}, u32[]{:S(2)}) collective-permute-start(bf16[128,192]{1,0:T(8,128)(2,1)S(1)} %get-tuple-element.144), channel_id=1, source_target_pairs={{0,3},{1,0},{2,1},{3,2},{4,7},{5,4},{6,5},{7,6},{8,11},{9,8},{10,9... | collective-permute-start | bytes 147464 | tf_op jit(solution)/shard_map/ppermute | solution.py:75
  170.6 32.5 %collective-permute-start.60 = (bf16[128,768]{1,0:T(8,128)(2,1)S(1)}, bf16[128,768]{1,0:T(8,128)(2,1)S(1)}, u32[]{:S(2)}, u32[]{:S(2)}) collective-permute-start(bf16[128,768]{1,0:T(8,128)(2,1)S(1)} %get-tuple-element.41), channel_id=1, source_target_pairs={{0,1},{1,2},{2,3},{3,0},{4,5},{5,6},{6,7},{7,4},{8,9},{9,10},{10,1... | collective-permute-start | bytes 589832 | tf_op jit(solution)/shard_map/ppermute | solution.py:70
  172.0 33.8 %collective-permute-start.59 = (bf16[128,768]{1,0:T(8,128)(2,1)S(1)}, bf16[128,768]{1,0:T(8,128)(2,1)S(1)}, u32[]{:S(2)}, u32[]{:S(2)}) collective-permute-start(bf16[128,768]{1,0:T(8,128)(2,1)S(1)} %get-tuple-element.41), channel_id=1, source_target_pairs={{0,2},{1,3},{2,0},{3,1},{4,6},{5,7},{6,4},{7,5},{8,10},{9,11},{10,... | collective-permute-start | bytes 589832 | tf_op jit(solution)/shard_map/ppermute | solution.py:70
  176.3 12.4 %collective-permute-start.27 = (bf16[128,768]{1,0:T(8,128)(2,1)S(1)}, bf16[128,768]{1,0:T(8,128)(2,1)S(1)}, u32[]{:S(2)}, u32[]{:S(2)}) collective-permute-start(bf16[128,768]{1,0:T(8,128)(2,1)S(1)} %get-tuple-element.114), channel_id=1, source_target_pairs={{0,1},{1,2},{2,3},{3,0},{4,5},{5,6},{6,7},{7,4},{8,9},{9,10},{10,1... | collective-permute-start | bytes 589832 | tf_op jit(solution)/shard_map/ppermute | solution.py:75
  177.8 13.3 %collective-permute-start.29 = (bf16[128,768]{1,0:T(8,128)(2,1)S(1)}, bf16[128,768]{1,0:T(8,128)(2,1)S(1)}, u32[]{:S(2)}, u32[]{:S(2)}) collective-permute-start(bf16[128,768]{1,0:T(8,128)(2,1)S(1)} %get-tuple-element.115), channel_id=1, source_target_pairs={{0,3},{1,0},{2,1},{3,2},{4,7},{5,4},{6,5},{7,6},{8,11},{9,8},{10,9... | collective-permute-start | bytes 589832 | tf_op jit(solution)/shard_map/ppermute | solution.py:75
  180.2 22.7 %collective-permute-start.28 = (bf16[128,768]{1,0:T(8,128)(2,1)S(1)}, bf16[128,768]{1,0:T(8,128)(2,1)S(1)}, u32[]{:S(2)}, u32[]{:S(2)}) collective-permute-start(bf16[128,768]{1,0:T(8,128)(2,1)S(1)} %get-tuple-element.116), channel_id=1, source_target_pairs={{0,2},{1,3},{2,0},{3,1},{4,6},{5,7},{6,4},{7,5},{8,10},{9,11},{10,... | collective-permute-start | bytes 589832 | tf_op jit(solution)/shard_map/ppermute | solution.py:75
  188.7 42.6 %copy-start.10 = (bf16[512,192]{1,0:T(8,128)(2,1)}, bf16[512,192]{1,0:T(8,128)(2,1)S(1)}, u32[]{:S(2)}) copy-start(bf16[512,192]{1,0:T(8,128)(2,1)S(1)} %add_convert_fusion.3) | copy-start | bytes 589828
  188.7 20.4 %collective-permute-start.58 = (bf16[128,768]{1,0:T(8,128)(2,1)S(1)}, bf16[128,768]{1,0:T(8,128)(2,1)S(1)}, u32[]{:S(2)}, u32[]{:S(2)}) collective-permute-start(bf16[128,768]{1,0:T(8,128)(2,1)S(1)} %get-tuple-element.41), channel_id=1, source_target_pairs={{0,3},{1,0},{2,1},{3,2},{4,7},{5,4},{6,5},{7,6},{8,11},{9,8},{10,9... | collective-permute-start | bytes 589832 | tf_op jit(solution)/shard_map/ppermute | solution.py:70
  191.1 31.8 %collective-permute-start.33 = (bf16[512,384]{1,0:T(8,128)(2,1)S(1)}, bf16[512,384]{1,0:T(8,128)(2,1)S(1)}, u32[]{:S(2)}, u32[]{:S(2)}) collective-permute-start(bf16[512,384]{1,0:T(8,128)(2,1)S(1)} %get-tuple-element.38), channel_id=1, source_target_pairs={{0,4},{4,0},{8,12},{12,8},{1,5},{5,1},{9,13},{13,9},{2,6},{6,2},{1... | collective-permute-start | bytes 1179656 | tf_op jit(solution)/shard_map/ppermute | solution.py:113
  202.9 7.7 %collective-permute-start.34 = (bf16[512,384]{1,0:T(8,128)(2,1)S(1)}, bf16[512,384]{1,0:T(8,128)(2,1)S(1)}, u32[]{:S(2)}, u32[]{:S(2)}) collective-permute-start(bf16[512,384]{1,0:T(8,128)(2,1)S(1)} %get-tuple-element.40), channel_id=1, source_target_pairs={{0,4},{4,0},{8,12},{12,8},{1,5},{5,1},{9,13},{13,9},{2,6},{6,2},{1... | collective-permute-start | bytes 1179656 | tf_op jit(solution)/shard_map/ppermute | solution.py:113
  203.1 19.7 %collective-permute-start.32 = (bf16[128,768]{1,0:T(8,128)(2,1)S(1)}, bf16[128,768]{1,0:T(8,128)(2,1)S(1)}, u32[]{:S(2)}, u32[]{:S(2)}) collective-permute-start(bf16[128,768]{1,0:T(8,128)(2,1)S(1)} %get-tuple-element.89), channel_id=1, source_target_pairs={{0,1},{1,2},{2,3},{3,0},{4,5},{5,6},{6,7},{7,4},{8,9},{9,10},{10,1... | collective-permute-start | bytes 589832 | tf_op jit(solution)/shard_map/ppermute | solution.py:70
  205.8 17.0 %collective-permute-start.31 = (bf16[128,768]{1,0:T(8,128)(2,1)S(1)}, bf16[128,768]{1,0:T(8,128)(2,1)S(1)}, u32[]{:S(2)}, u32[]{:S(2)}) collective-permute-start(bf16[128,768]{1,0:T(8,128)(2,1)S(1)} %get-tuple-element.89), channel_id=1, source_target_pairs={{0,2},{1,3},{2,0},{3,1},{4,6},{5,7},{6,4},{7,5},{8,10},{9,11},{10,... | collective-permute-start | bytes 589832 | tf_op jit(solution)/shard_map/ppermute | solution.py:70
  209.2 9.9 %collective-permute-start.30 = (bf16[128,768]{1,0:T(8,128)(2,1)S(1)}, bf16[128,768]{1,0:T(8,128)(2,1)S(1)}, u32[]{:S(2)}, u32[]{:S(2)}) collective-permute-start(bf16[128,768]{1,0:T(8,128)(2,1)S(1)} %get-tuple-element.89), channel_id=1, source_target_pairs={{0,3},{1,0},{2,1},{3,2},{4,7},{5,4},{6,5},{7,6},{8,11},{9,8},{10,9... | collective-permute-start | bytes 589832 | tf_op jit(solution)/shard_map/ppermute | solution.py:70
  210.7 12.1 %collective-permute-start.35 = (bf16[512,384]{1,0:T(8,128)(2,1)S(1)}, bf16[512,384]{1,0:T(8,128)(2,1)S(1)}, u32[]{:S(2)}, u32[]{:S(2)}) collective-permute-start(bf16[512,384]{1,0:T(8,128)(2,1)S(1)} %add_convert_fusion.2), channel_id=1, source_target_pairs={{0,8},{4,12},{8,0},{12,4},{1,9},{5,13},{9,1},{13,5},{2,10},{6,14},... | collective-permute-start | bytes 1179656 | tf_op jit(solution)/shard_map/ppermute | solution.py:113
  224.9 10.1 %collective-permute-start.36 = (bf16[128,768]{1,0:T(8,128)(2,1)S(1)}, bf16[128,768]{1,0:T(8,128)(2,1)S(1)}, u32[]{:S(2)}, u32[]{:S(2)}) collective-permute-start(bf16[128,768]{1,0:T(8,128)(2,1)S(1)} %get-tuple-element.111), channel_id=1, source_target_pairs={{0,1},{1,2},{2,3},{3,0},{4,5},{5,6},{6,7},{7,4},{8,9},{9,10},{10,1... | collective-permute-start | bytes 589832 | tf_op jit(solution)/shard_map/ppermute | solution.py:75
  229.7 9.5 %collective-permute-start.38 = (bf16[128,768]{1,0:T(8,128)(2,1)S(1)}, bf16[128,768]{1,0:T(8,128)(2,1)S(1)}, u32[]{:S(2)}, u32[]{:S(2)}) collective-permute-start(bf16[128,768]{1,0:T(8,128)(2,1)S(1)} %get-tuple-element.112), channel_id=1, source_target_pairs={{0,3},{1,0},{2,1},{3,2},{4,7},{5,4},{6,5},{7,6},{8,11},{9,8},{10,9... | collective-permute-start | bytes 589832 | tf_op jit(solution)/shard_map/ppermute | solution.py:75
  229.7 16.5 %collective-permute-start.37 = (bf16[128,768]{1,0:T(8,128)(2,1)S(1)}, bf16[128,768]{1,0:T(8,128)(2,1)S(1)}, u32[]{:S(2)}, u32[]{:S(2)}) collective-permute-start(bf16[128,768]{1,0:T(8,128)(2,1)S(1)} %get-tuple-element.113), channel_id=1, source_target_pairs={{0,2},{1,3},{2,0},{3,1},{4,6},{5,7},{6,4},{7,5},{8,10},{9,11},{10,... | collective-permute-start | bytes 589832 | tf_op jit(solution)/shard_map/ppermute | solution.py:75
  249.1 13.0 %collective-permute-start.39 = (bf16[144,768]{1,0:T(8,128)(2,1)S(1)}, bf16[144,768]{1,0:T(8,128)(2,1)S(1)}, u32[]{:S(2)}, u32[]{:S(2)}) collective-permute-start(bf16[144,768]{1,0:T(8,128)(2,1)S(1)} %concatenate.143), channel_id=1, source_target_pairs={{0,3},{1,0},{2,1},{3,2},{4,7},{5,4},{6,5},{7,6},{8,11},{9,8},{10,9... | collective-permute-start | bytes 663560 | tf_op jit(solution)/shard_map/ppermute | solution.py:70
  252.8 17.7 %collective-permute-start.41 = (bf16[144,768]{1,0:T(8,128)(2,1)S(1)}, bf16[144,768]{1,0:T(8,128)(2,1)S(1)}, u32[]{:S(2)}, u32[]{:S(2)}) collective-permute-start(bf16[144,768]{1,0:T(8,128)(2,1)S(1)} %concatenate.143), channel_id=1, source_target_pairs={{0,1},{1,2},{2,3},{3,0},{4,5},{5,6},{6,7},{7,4},{8,9},{9,10},{10,1... | collective-permute-start | bytes 663560 | tf_op jit(solution)/shard_map/ppermute | solution.py:70
  252.8 17.7 %collective-permute-start.40 = (bf16[144,768]{1,0:T(8,128)(2,1)S(1)}, bf16[144,768]{1,0:T(8,128)(2,1)S(1)}, u32[]{:S(2)}, u32[]{:S(2)}) collective-permute-start(bf16[144,768]{1,0:T(8,128)(2,1)S(1)} %concatenate.143), channel_id=1, source_target_pairs={{0,2},{1,3},{2,0},{3,1},{4,6},{5,7},{6,4},{7,5},{8,10},{9,11},{10,... | collective-permute-start | bytes 663560 | tf_op jit(solution)/shard_map/ppermute | solution.py:70
  270.8 3.9 collective-permute-start.42
  272.3 3.5 collective-permute-start.43
  282.9 13.6 %collective-permute-start.50 = (bf16[672,384]{1,0:T(8,128)(2,1)S(1)}, bf16[672,384]{1,0:T(8,128)(2,1)S(1)}, u32[]{:S(2)}, u32[]{:S(2)}) collective-permute-start(bf16[672,384]{1,0:T(8,128)(2,1)S(1)} %dynamic-slice_convert_fusion), channel_id=1, source_target_pairs={{0,4},{4,0},{8,12},{12,8},{1,5},{5,1},{9,13},{13,9},{2,6},{6,2},{1... | collective-permute-start | bytes 1548296 | tf_op jit(solution)/shard_map/ppermute | solution.py:113
  285.9 6.4 %collective-permute-start.44 = (bf16[128,160]{0,1:T(8,128)(2,1)S(1)}, bf16[128,160]{0,1:T(8,128)(2,1)S(1)}, u32[]{:S(2)}, u32[]{:S(2)}) collective-permute-start(bf16[128,160]{0,1:T(8,128)(2,1)S(1)} %get-tuple-element.124), channel_id=1, source_target_pairs={{0,1},{1,2},{2,3},{3,0},{4,5},{5,6},{6,7},{7,4},{8,9},{9,10},{10,1... | collective-permute-start | bytes 122888 | tf_op jit(solution)/shard_map/ppermute | solution.py:75
  285.9 7.3 %collective-permute-start.45 = (bf16[128,160]{0,1:T(8,128)(2,1)S(1)}, bf16[128,160]{0,1:T(8,128)(2,1)S(1)}, u32[]{:S(2)}, u32[]{:S(2)}) collective-permute-start(bf16[128,160]{0,1:T(8,128)(2,1)S(1)} %get-tuple-element.125), channel_id=1, source_target_pairs={{0,2},{1,3},{2,0},{3,1},{4,6},{5,7},{6,4},{7,5},{8,10},{9,11},{10,... | collective-permute-start | bytes 122888 | tf_op jit(solution)/shard_map/ppermute | solution.py:75
  289.1 4.2 %collective-permute-start.46 = (bf16[128,160]{0,1:T(8,128)(2,1)S(1)}, bf16[128,160]{0,1:T(8,128)(2,1)S(1)}, u32[]{:S(2)}, u32[]{:S(2)}) collective-permute-start(bf16[128,160]{0,1:T(8,128)(2,1)S(1)} %get-tuple-element.126), channel_id=1, source_target_pairs={{0,3},{1,0},{2,1},{3,2},{4,7},{5,4},{6,5},{7,6},{8,11},{9,8},{10,9... | collective-permute-start | bytes 122888 | tf_op jit(solution)/shard_map/ppermute | solution.py:75
  293.4 8.9 %collective-permute-start.47 = (bf16[128,160]{0,1:T(8,128)(2,1)S(1)}, bf16[128,160]{0,1:T(8,128)(2,1)S(1)}, u32[]{:S(2)}, u32[]{:S(2)}) collective-permute-start(bf16[128,160]{0,1:T(8,128)(2,1)S(1)} %get-tuple-element.81), channel_id=1, source_target_pairs={{0,3},{1,0},{2,1},{3,2},{4,7},{5,4},{6,5},{7,6},{8,11},{9,8},{10,9... | collective-permute-start | bytes 122888 | tf_op jit(solution)/shard_map/ppermute | solution.py:70
  296.7 7.7 %collective-permute-start.51 = (bf16[168,384]{1,0:T(8,128)(2,1)S(1)}, bf16[168,384]{1,0:T(8,128)(2,1)S(1)}, u32[]{:S(2)}, u32[]{:S(2)}) collective-permute-start(bf16[168,384]{1,0:T(8,128)(2,1)S(1)} %get-tuple-element.108), channel_id=1, source_target_pairs={{0,8},{4,12},{8,0},{12,4},{16,24},{20,28},{24,16},{28,20},{1,9},{5... | collective-permute-start | bytes 387080 | tf_op jit(solution)/shard_map/ppermute | solution.py:145
  296.8 7.6 %collective-permute-start.53 = (bf16[168,384]{1,0:T(8,128)(2,1)S(1)}, bf16[168,384]{1,0:T(8,128)(2,1)S(1)}, u32[]{:S(2)}, u32[]{:S(2)}) collective-permute-start(bf16[168,384]{1,0:T(8,128)(2,1)S(1)} %get-tuple-element.109), channel_id=1, source_target_pairs={{0,24},{4,28},{8,16},{12,20},{16,8},{20,12},{24,0},{28,4},{1,25},{... | collective-permute-start | bytes 387080 | tf_op jit(solution)/shard_map/ppermute | solution.py:145
  300.0 5.7 %collective-permute-start.52 = (bf16[168,384]{1,0:T(8,128)(2,1)S(1)}, bf16[168,384]{1,0:T(8,128)(2,1)S(1)}, u32[]{:S(2)}, u32[]{:S(2)}) collective-permute-start(bf16[168,384]{1,0:T(8,128)(2,1)S(1)} %get-tuple-element.110), channel_id=1, source_target_pairs={{0,16},{4,20},{8,24},{12,28},{16,0},{20,4},{24,8},{28,12},{1,17},{... | collective-permute-start | bytes 387080 | tf_op jit(solution)/shard_map/ppermute | solution.py:145
  302.1 7.3 %collective-permute-start.49 = (bf16[128,160]{0,1:T(8,128)(2,1)S(1)}, bf16[128,160]{0,1:T(8,128)(2,1)S(1)}, u32[]{:S(2)}, u32[]{:S(2)}) collective-permute-start(bf16[128,160]{0,1:T(8,128)(2,1)S(1)} %get-tuple-element.81), channel_id=1, source_target_pairs={{0,1},{1,2},{2,3},{3,0},{4,5},{5,6},{6,7},{7,4},{8,9},{9,10},{10,1... | collective-permute-start | bytes 122888 | tf_op jit(solution)/shard_map/ppermute | solution.py:70
  302.3 7.0 %collective-permute-start.48 = (bf16[128,160]{0,1:T(8,128)(2,1)S(1)}, bf16[128,160]{0,1:T(8,128)(2,1)S(1)}, u32[]{:S(2)}, u32[]{:S(2)}) collective-permute-start(bf16[128,160]{0,1:T(8,128)(2,1)S(1)} %get-tuple-element.81), channel_id=1, source_target_pairs={{0,2},{1,3},{2,0},{3,1},{4,6},{5,7},{6,4},{7,5},{8,10},{9,11},{10,... | collective-permute-start | bytes 122888 | tf_op jit(solution)/shard_map/ppermute | solution.py:70
  305.8 10.0 %collective-permute-start.56 = (bf16[168,384]{1,0:T(8,128)(2,1)S(1)}, bf16[168,384]{1,0:T(8,128)(2,1)S(1)}, u32[]{:S(2)}, u32[]{:S(2)}) collective-permute-start(bf16[168,384]{1,0:T(8,128)(2,1)S(1)} %add_convert_fusion.7), channel_id=1, source_target_pairs={{0,24},{4,28},{8,16},{12,20},{16,8},{20,12},{24,0},{28,4},{1,25},{... | collective-permute-start | bytes 387080 | tf_op jit(solution)/shard_map/ppermute | solution.py:150
  307.3 12.1 %collective-permute-start.55 = (bf16[168,384]{1,0:T(8,128)(2,1)S(1)}, bf16[168,384]{1,0:T(8,128)(2,1)S(1)}, u32[]{:S(2)}, u32[]{:S(2)}) collective-permute-start(bf16[168,384]{1,0:T(8,128)(2,1)S(1)} %add_convert_fusion.7), channel_id=1, source_target_pairs={{0,16},{4,20},{8,24},{12,28},{16,0},{20,4},{24,8},{28,12},{1,17},{... | collective-permute-start | bytes 387080 | tf_op jit(solution)/shard_map/ppermute | solution.py:150
  307.8 11.6 %collective-permute-start.54 = (bf16[168,384]{1,0:T(8,128)(2,1)S(1)}, bf16[168,384]{1,0:T(8,128)(2,1)S(1)}, u32[]{:S(2)}, u32[]{:S(2)}) collective-permute-start(bf16[168,384]{1,0:T(8,128)(2,1)S(1)} %add_convert_fusion.7), channel_id=1, source_target_pairs={{0,8},{4,12},{8,0},{12,4},{16,24},{20,28},{24,16},{28,20},{1,9},{5... | collective-permute-start | bytes 387080 | tf_op jit(solution)/shard_map/ppermute | solution.py:150
  319.7 2.1 collective-permute-start.57
  (104 other events, 966.0 us)
Sparse Core Ops, SparseCore 0:
  302.2 75.5 all-reduce.3
